TPU v7x, 32 devices: a whole 2x2x4 slice. The times are simulated.
32 devices in a mesh: seq: 4 (over x, core), batch: 8 (over z, y).
Axes of the slice: x: 2, y: 2, z: 4, core: 2. Of those that a mesh axis runs over, the one named last changes fastest.
Arguments:
- tokens: bfloat16 [8, 512, 2048], P('batch', 'seq'), may hold values from -6 to 6
- lengths: int32 [8], P('batch'), may hold values from 1 to 512, 2560 in all
- cotangent: bfloat16 [8, 512, 2048], P('batch', 'seq'), may hold values from -6 to 6
- input_proj: bfloat16 [2048, 2560], P(('seq', 'batch')), may hold values from -0.125 to 0.125
- branch_proj: bfloat16 [2048, 2560], P(('seq', 'batch')), may hold values from -0.125 to 0.125
- output_proj: bfloat16 [2560, 2048], P(('seq', 'batch')), may hold values from -0.3125 to 0.3125
- recur_gate: bfloat16 [2560, 256], P(('seq', 'batch')), may hold values from -0.375 to 0.375
- inlet_gate: bfloat16 [2560, 256], P(('seq', 'batch')), may hold values from -0.375 to 0.375
- conv_kernel: bfloat16 [4, 2560], P(None, ('seq', 'batch')), may hold values from -3 to 3
- conv_bias: bfloat16 [2560], P(('seq', 'batch')), may hold values from -3 to 3
- recur_bias: bfloat16 [2560], P(('seq', 'batch')), may hold values from -4 to 4
- inlet_bias: bfloat16 [2560], P(('seq', 'batch')), may hold values from -4 to 4
- decay_param: bfloat16 [2560], P(('seq', 'batch')), may hold values from -12 to -4
- mixer_gain: bfloat16 [2048], P(('seq', 'batch')), may hold values from 0.5 to 1.5
- feed_gain: bfloat16 [2048], P(('seq', 'batch')), may hold values from 0.5 to 1.5
- feed_gate: bfloat16 [2048, 6144], P('batch', 'seq'), may hold values from -0.125 to 0.125
- feed_up: bfloat16 [2048, 6144], P('batch', 'seq'), may hold values from -0.125 to 0.125
- feed_down: bfloat16 [6144, 2048], P('seq', 'batch'), may hold values from -0.078125 to 0.078125
Outputs:
- output: bfloat16 [8, 512, 2048], P('batch', 'seq')
- grad_tokens: float32 [8, 512, 2048], P('batch', 'seq')
- grad_input_proj: float32 [2048, 2560], P(('seq', 'batch'))
- grad_branch_proj: float32 [2048, 2560], P(('seq', 'batch'))
- grad_output_proj: float32 [2560, 2048], P(('seq', 'batch'))
- grad_recur_gate: float32 [2560, 256], P(('seq', 'batch'))
- grad_inlet_gate: float32 [2560, 256], P(('seq', 'batch'))
- grad_conv_kernel: float32 [4, 2560], P(None, ('seq', 'batch'))
- grad_conv_bias: float32 [2560], P(('seq', 'batch'))
- grad_recur_bias: float32 [2560], P(('seq', 'batch'))
- grad_inlet_bias: float32 [2560], P(('seq', 'batch'))
- grad_decay_param: float32 [2560], P(('seq', 'batch'))
- grad_mixer_gain: float32 [2048], P(('seq', 'batch'))
- grad_feed_gain: float32 [2048], P(('seq', 'batch'))
- grad_feed_gate: float32 [2048, 6144], P('batch', 'seq')
- grad_feed_up: float32 [2048, 6144], P('batch', 'seq')
- grad_feed_down: float32 [6144, 2048], P('seq', 'batch')
All inputs are finite; a program needn't handle non-finite values. No bound on the sum of `lengths` on one device may be relied on, other than what follows from the above.
Results may differ from a plain program's by a relative error of at most 0.014.
Values may be sent and summed in bfloat16 or wider, within the bound.
No kernel may reach another device: no remote copies, remote signals or barrier semaphores. Data moves between devices by JAX's collectives and lax.ppermute only.
A program may use at most 320 MiB of HBM per device.

v0:
```python
import jax
import jax.numpy as jnp
from jax import lax
from jax.sharding import PartitionSpec as P

NH = 10
HB = 256


epsilon = 1e-06


def from_behind(block, axis, distance):
    devices = range(lax.axis_size(axis))
    route = [(i - distance, i) for i in devices if i - distance in devices]
    return lax.ppermute(block, axis, route)


def entering(part, axis, combine, identity, reverse):
    count = lax.axis_size(axis)
    place = lax.axis_index(axis)
    ahead = count - 1 - place if reverse else place
    gathered = jax.tree.map(lambda a: lax.all_gather(a, axis), part)
    state = jax.tree.map(lambda a, e: jnp.zeros_like(a) + jnp.asarray(e, a.dtype), part, identity)

    def one(step, state):
        source = count - 1 - step if reverse else step
        return combine(
            state, jax.tree.map(lambda a: lax.dynamic_index_in_dim(a, source, 0, False), gathered)
        )

    return lax.fori_loop(0, ahead, one, state)


def affine_join(earlier, later):
    return (earlier[0] * later[0], later[0] * earlier[1] + later[1])


def gelu_tanh(values):
    return jax.nn.gelu(values, approximate=True)


def rms_factor(values):
    return lax.rsqrt(jnp.mean(values * values, axis=-1, keepdims=True) + epsilon)


def norm_backward(grad_normed, scaled, factor, gain):
    weighted = grad_normed * gain
    inner_mean = jnp.mean(weighted * scaled, axis=-1, keepdims=True)
    return (factor * (weighted - scaled * inner_mean), jnp.sum(grad_normed * scaled, axis=0))


def conv_gates(
    extended, kernel, bias_conv, recur_full, inlet_full, bias_recur, bias_inlet, channel_rate
):
    length = extended.shape[0] - 3
    kernel_wide = kernel.astype(jnp.float32)
    extended_wide = extended.astype(jnp.float32)
    convolved = bias_conv.astype(jnp.float32) + kernel_wide[0] * extended_wide[3 : 3 + length]
    for offset in range(1, 4):
        convolved = (
            convolved + kernel_wide[offset] * extended_wide[3 - offset : 3 - offset + length]
        )
    conv_low = convolved.astype(jnp.bfloat16)
    head_view = conv_low.reshape(length, NH, HB)
    recur_pre = jnp.einsum(
        "thi,hij->thj",
        head_view,
        recur_full.reshape(NH, HB, HB),
        preferred_element_type=jnp.float32,
    ).reshape(length, NH * HB) + bias_recur.astype(jnp.float32)
    inlet_pre = jnp.einsum(
        "thi,hij->thj",
        head_view,
        inlet_full.reshape(NH, HB, HB),
        preferred_element_type=jnp.float32,
    ).reshape(length, NH * HB) + bias_inlet.astype(jnp.float32)
    recurrence = jax.nn.sigmoid(recur_pre)
    inlets = jax.nn.sigmoid(inlet_pre)
    log_decay = -8.0 * recurrence * channel_rate
    decays = jnp.exp(log_decay)
    scaling = jnp.sqrt(-jnp.expm1(2.0 * log_decay))
    conv_value = conv_low.astype(jnp.float32)
    cumulative, local_state = lax.associative_scan(
        affine_join, (decays, scaling * inlets * conv_value), axis=0
    )
    return (conv_value, head_view, recurrence, inlets, decays, scaling, cumulative, local_state)


def on_device(
    tokens,
    lengths,
    cotangent,
    input_proj,
    branch_proj,
    output_proj,
    recur_gate,
    inlet_gate,
    conv_kernel,
    conv_bias,
    recur_bias,
    inlet_bias,
    decay_param,
    mixer_gain,
    feed_gain,
    feed_gate,
    feed_up,
    feed_down,
):
    row_count = tokens.shape[1]
    positions = lax.axis_index("seq") * row_count + jnp.arange(row_count, dtype=jnp.int32)
    validity = (positions < lengths[0]).astype(jnp.float32)[:, None]
    gathered = (
        lax.all_gather(input_proj, ("seq", "batch"), axis=0, tiled=True),
        lax.all_gather(branch_proj, ("seq", "batch"), axis=0, tiled=True),
        lax.all_gather(output_proj, ("seq", "batch"), axis=0, tiled=True),
        lax.all_gather(recur_gate, ("seq", "batch"), axis=0, tiled=True),
        lax.all_gather(inlet_gate, ("seq", "batch"), axis=0, tiled=True),
        lax.all_gather(conv_kernel, ("seq", "batch"), axis=1, tiled=True),
        lax.all_gather(conv_bias, ("seq", "batch"), axis=0, tiled=True),
        lax.all_gather(recur_bias, ("seq", "batch"), axis=0, tiled=True),
        lax.all_gather(inlet_bias, ("seq", "batch"), axis=0, tiled=True),
        lax.all_gather(decay_param, ("seq", "batch"), axis=0, tiled=True),
        lax.all_gather(mixer_gain, ("seq", "batch"), axis=0, tiled=True),
        lax.all_gather(feed_gain, ("seq", "batch"), axis=0, tiled=True),
    )
    (
        input_full,
        branch_full,
        output_full,
        recur_full,
        inlet_full,
        kernel_full,
        bias_conv,
        bias_recur,
        bias_inlet,
        param_full,
        gain_mixer,
        gain_feed,
    ) = gathered
    param_wide = param_full.astype(jnp.float32)
    channel_rate = jax.nn.softplus(param_wide)
    gain_one = gain_mixer.astype(jnp.float32)
    gain_two = gain_feed.astype(jnp.float32)
    token_rows = tokens[0].astype(jnp.float32)
    factor_one = rms_factor(token_rows)
    scaled_one = token_rows * factor_one
    normed = (scaled_one * gain_one).astype(jnp.bfloat16)
    branch = jnp.dot(normed, branch_full, preferred_element_type=jnp.float32)
    inner_proj = jnp.dot(normed, input_full, preferred_element_type=jnp.float32).astype(
        jnp.bfloat16
    )
    rim_rows = from_behind(inner_proj[row_count - 3 :], "seq", 1)
    extended = jnp.concatenate([rim_rows, inner_proj], axis=0)
    conv_value, head_view, recurrence, inlets, decays, scaling, cumulative, local_state = (
        conv_gates(
            extended,
            kernel_full,
            bias_conv,
            recur_full,
            inlet_full,
            bias_recur,
            bias_inlet,
            channel_rate,
        )
    )
    carried_in = entering(
        (cumulative[row_count - 1], local_state[row_count - 1]),
        "seq",
        affine_join,
        (jnp.ones_like(cumulative[0]), jnp.zeros_like(local_state[0])),
        False,
    )
    state_in = carried_in[1]
    states = local_state + cumulative * state_in
    gate_values = gelu_tanh(branch)
    mixed_in = (gate_values * states).astype(jnp.bfloat16)
    mix = jnp.dot(mixed_in, output_full, preferred_element_type=jnp.float32)
    middle = token_rows + validity * mix
    factor_two = rms_factor(middle)
    scaled_two = middle * factor_two
    normed_two = (scaled_two * gain_two).astype(jnp.bfloat16)
    gate_local, lin_local, down_local = (
        lax.all_gather(feed_gate, "batch", axis=0, tiled=True),
        lax.all_gather(feed_up, "batch", axis=0, tiled=True),
        lax.all_gather(feed_down, "batch", axis=1, tiled=True),
    )
    all_rows = lax.all_gather(normed_two, "seq", axis=0, tiled=True)
    feed_pre = jnp.dot(all_rows, gate_local, preferred_element_type=jnp.float32)
    feed_lin = jnp.dot(all_rows, lin_local, preferred_element_type=jnp.float32)
    feed_act, gelu_pull = jax.vjp(gelu_tanh, feed_pre)
    hidden = (feed_act * feed_lin).astype(jnp.bfloat16)
    feed_out = lax.psum_scatter(
        jnp.dot(hidden, down_local, preferred_element_type=jnp.float32),
        "seq",
        scatter_dimension=0,
        tiled=True,
    )
    output = (middle + validity * feed_out).astype(jnp.bfloat16)[None]
    grad_out = cotangent[0].astype(jnp.float32)
    grad_feed = (validity * grad_out).astype(jnp.bfloat16)
    grad_all = lax.all_gather(grad_feed, "seq", axis=0, tiled=True)
    grad_hidden = jnp.dot(grad_all, down_local.T, preferred_element_type=jnp.float32)
    grad_pre = gelu_pull(grad_hidden * feed_lin)[0].astype(jnp.bfloat16)
    grad_lin = (grad_hidden * feed_act).astype(jnp.bfloat16)
    grad_rows = jnp.dot(grad_pre, gate_local.T, preferred_element_type=jnp.float32) + jnp.dot(
        grad_lin, lin_local.T, preferred_element_type=jnp.float32
    )
    grad_normed_two = lax.psum_scatter(grad_rows, "seq", scatter_dimension=0, tiled=True)
    feed_grads = (
        lax.psum_scatter(
            jnp.einsum("td,tf->df", all_rows, grad_pre, preferred_element_type=jnp.float32),
            "batch",
            scatter_dimension=0,
            tiled=True,
        ),
        lax.psum_scatter(
            jnp.einsum("td,tf->df", all_rows, grad_lin, preferred_element_type=jnp.float32),
            "batch",
            scatter_dimension=0,
            tiled=True,
        ),
        lax.psum_scatter(
            jnp.einsum("tf,td->fd", hidden, grad_all, preferred_element_type=jnp.float32),
            "batch",
            scatter_dimension=1,
            tiled=True,
        ),
    )
    grad_mid_norm, grad_gain_feed = norm_backward(grad_normed_two, scaled_two, factor_two, gain_two)
    grad_middle = grad_out + grad_mid_norm
    regathered = (
        lax.all_gather(input_proj, ("seq", "batch"), axis=0, tiled=True),
        lax.all_gather(branch_proj, ("seq", "batch"), axis=0, tiled=True),
        lax.all_gather(output_proj, ("seq", "batch"), axis=0, tiled=True),
        lax.all_gather(recur_gate, ("seq", "batch"), axis=0, tiled=True),
        lax.all_gather(inlet_gate, ("seq", "batch"), axis=0, tiled=True),
        lax.all_gather(conv_kernel, ("seq", "batch"), axis=1, tiled=True),
    )
    back_input, back_branch, back_output, back_recur, back_inlet, back_kernel = regathered
    grad_mix = (validity * grad_middle).astype(jnp.bfloat16)
    grad_output_full = jnp.einsum(
        "tr,td->rd", mixed_in, grad_mix, preferred_element_type=jnp.float32
    )
    grad_mixed = jnp.dot(grad_mix, back_output.T, preferred_element_type=jnp.float32)
    grad_branch = jax.vjp(gelu_tanh, branch)[1](grad_mixed * states)[0].astype(jnp.bfloat16)
    grad_states = grad_mixed * gate_values
    next_decays = jnp.concatenate([decays[1:], jnp.ones_like(decays[:1])], axis=0)
    back_cum, back_local = lax.associative_scan(
        affine_join, (next_decays, grad_states), axis=0, reverse=True
    )
    incoming = entering(
        (decays[0] * back_cum[0], decays[0] * back_local[0]),
        "seq",
        affine_join,
        (jnp.ones_like(back_cum[0]), jnp.zeros_like(back_local[0])),
        True,
    )[1]
    carried = back_local + back_cum * incoming
    previous = jnp.concatenate([state_in[None], states[:-1]], axis=0)
    drive_grad = carried * conv_value
    grad_log = carried * previous * decays - drive_grad * inlets * decays * decays / scaling
    grad_recur_pre = grad_log * (-8.0 * channel_rate) * recurrence * (1.0 - recurrence)
    grad_inlet_pre = drive_grad * scaling * inlets * (1.0 - inlets)
    grad_param = jnp.sum(grad_log * (-8.0 * recurrence), axis=0) * jax.nn.sigmoid(param_wide)
    grad_bias_recur = jnp.sum(grad_recur_pre, axis=0)
    grad_bias_inlet = jnp.sum(grad_inlet_pre, axis=0)
    rounded_recur = grad_recur_pre.astype(jnp.bfloat16).reshape(row_count, NH, HB)
    rounded_inlet = grad_inlet_pre.astype(jnp.bfloat16).reshape(row_count, NH, HB)
    grad_recur_full = jnp.einsum(
        "thi,thj->hij", head_view, rounded_recur, preferred_element_type=jnp.float32
    ).reshape(NH * HB, HB)
    grad_inlet_full = jnp.einsum(
        "thi,thj->hij", head_view, rounded_inlet, preferred_element_type=jnp.float32
    ).reshape(NH * HB, HB)
    grad_conv = carried * scaling * inlets
    grad_conv = grad_conv + jnp.einsum(
        "thj,hij->thi",
        rounded_recur,
        back_recur.reshape(NH, HB, HB),
        preferred_element_type=jnp.float32,
    ).reshape(row_count, NH * HB)
    grad_conv = grad_conv + jnp.einsum(
        "thj,hij->thi",
        rounded_inlet,
        back_inlet.reshape(NH, HB, HB),
        preferred_element_type=jnp.float32,
    ).reshape(row_count, NH * HB)
    ahead = from_behind(grad_conv[:3], "seq", -1)
    extended_back = jnp.concatenate([grad_conv, ahead], axis=0)
    kernel_wide = back_kernel.astype(jnp.float32)
    grad_inner = kernel_wide[0] * extended_back[0:row_count]
    for offset in range(1, 4):
        grad_inner = grad_inner + kernel_wide[offset] * extended_back[offset : offset + row_count]
    grad_inner = grad_inner.astype(jnp.bfloat16)
    extended_wide = extended.astype(jnp.float32)
    grad_kernel = jnp.stack(
        [
            jnp.sum(grad_conv * extended_wide[3 - offset : 3 - offset + row_count], axis=0)
            for offset in range(4)
        ],
        axis=0,
    )
    grad_bias_conv = jnp.sum(grad_conv, axis=0)
    grad_input_full = jnp.einsum(
        "td,tr->dr", normed, grad_inner, preferred_element_type=jnp.float32
    )
    grad_branch_full = jnp.einsum(
        "td,tr->dr", normed, grad_branch, preferred_element_type=jnp.float32
    )
    grad_normed = jnp.dot(grad_inner, back_input.T, preferred_element_type=jnp.float32) + jnp.dot(
        grad_branch, back_branch.T, preferred_element_type=jnp.float32
    )
    grad_token_norm, grad_gain_mixer = norm_backward(grad_normed, scaled_one, factor_one, gain_one)
    grad_tokens = (grad_middle + grad_token_norm)[None]
    mixer_grads = (
        lax.psum_scatter(grad_input_full, ("seq", "batch"), scatter_dimension=0, tiled=True),
        lax.psum_scatter(grad_branch_full, ("seq", "batch"), scatter_dimension=0, tiled=True),
        lax.psum_scatter(grad_output_full, ("seq", "batch"), scatter_dimension=0, tiled=True),
        lax.psum_scatter(grad_recur_full, ("seq", "batch"), scatter_dimension=0, tiled=True),
        lax.psum_scatter(grad_inlet_full, ("seq", "batch"), scatter_dimension=0, tiled=True),
        lax.psum_scatter(grad_kernel, ("seq", "batch"), scatter_dimension=1, tiled=True),
        lax.psum_scatter(grad_bias_conv, ("seq", "batch"), scatter_dimension=0, tiled=True),
        lax.psum_scatter(grad_bias_recur, ("seq", "batch"), scatter_dimension=0, tiled=True),
        lax.psum_scatter(grad_bias_inlet, ("seq", "batch"), scatter_dimension=0, tiled=True),
        lax.psum_scatter(grad_param, ("seq", "batch"), scatter_dimension=0, tiled=True),
        lax.psum_scatter(grad_gain_mixer, ("seq", "batch"), scatter_dimension=0, tiled=True),
        lax.psum_scatter(grad_gain_feed, ("seq", "batch"), scatter_dimension=0, tiled=True),
    )
    return (
        output,
        grad_tokens,
        mixer_grads[0],
        mixer_grads[1],
        mixer_grads[2],
        mixer_grads[3],
        mixer_grads[4],
        mixer_grads[5],
        mixer_grads[6],
        mixer_grads[7],
        mixer_grads[8],
        mixer_grads[9],
        mixer_grads[10],
        mixer_grads[11],
        feed_grads[0],
        feed_grads[1],
        feed_grads[2],
    )


def solution(mesh):
    in_specs = (
        P("batch", "seq", None),
        P("batch"),
        P("batch", "seq", None),
        P(("seq", "batch"), None),
        P(("seq", "batch"), None),
        P(("seq", "batch"), None),
        P(("seq", "batch"), None),
        P(("seq", "batch"), None),
        P(None, ("seq", "batch")),
        P(("seq", "batch")),
        P(("seq", "batch")),
        P(("seq", "batch")),
        P(("seq", "batch")),
        P(("seq", "batch")),
        P(("seq", "batch")),
        P("batch", "seq"),
        P("batch", "seq"),
        P("seq", "batch"),
    )
    out_specs = (
        P("batch", "seq", None),
        P("batch", "seq", None),
        P(("seq", "batch"), None),
        P(("seq", "batch"), None),
        P(("seq", "batch"), None),
        P(("seq", "batch"), None),
        P(("seq", "batch"), None),
        P(None, ("seq", "batch")),
        P(("seq", "batch")),
        P(("seq", "batch")),
        P(("seq", "batch")),
        P(("seq", "batch")),
        P(("seq", "batch")),
        P(("seq", "batch")),
        P("batch", "seq"),
        P("batch", "seq"),
        P("seq", "batch"),
    )
    return jax.shard_map(
        on_device, mesh=mesh, in_specs=in_specs, out_specs=out_specs, check_vma=False
    )
```

profile of v0, /device:TPU:1, one launch (start us, length us, event | category | flops | bytes accessed | tf_op | source)
XLA Modules:
  0.0 3517.8 jit_solution(8992309451628467163)
XLA Ops:
  12.8 42.5 %all-reduce.71 = (bf16[2560]{0:T(1024)(128)(2,1)S(1)}, bf16[2048]{0:T(1024)(128)(2,1)S(1)}, bf16[2560]{0:T(1024)(128)(2,1)S(1)}, bf16[2560]{0:T(1024)(128)(2,1)S...) all-reduce(bf16[2560]{0:T(1024)(128)(2,1)S(1)} %dynamic-update-slic, ...), channel_id=1, replica_groups=mesh['seq'=4,'batch'=8] {'seq','batch'}, use_global_device_ids=true, to_apply=%add.61 | all-reduce | flops 14336 | bytes 57344
  55.6 61.7 %all-gather = bf16[32,80,4]{1,2,0:T(4,128)(2,1)S(1)} all-gather(bf16[1,80,4]{1,2,0:T(4,128)(2,1)S(1)} %bitcast.140), channel_id=1, replica_groups=mesh['seq'=4,'batch'=8] {'seq','batch'}, dimensions={0}, use_global_device_ids=true | all-gather | bytes 21120 | tf_op jit(solution)/shard_map/all_gather | solution.py:119
  118.3 5.6 convolution_convert_fusion
  123.9 7.6 collective-permute-start
  133.8 23.0 all-gather.20.cloned.1.call-done
  164.1 49.0 %all-gather.22.cloned.1.call-done = bf16[2560,256]{1,0:T(8,128)(2,1)} async-done(((bf16[80,256]{1,0:T(8,128)(2,1)}), bf16[2560,256]{1,0:T(8,128)(2,1)}) %all-gather.22.cloned.1.call-update) | async-done | bytes 1310736 | tf_op jit(solution)/shard_map/all_gather | solution.py:118
  379.0 5.3 all-gather.2
  402.8 9.3 multiply_convert_fusion.2
  412.1 6.0 multiply_reduce_fusion.7
  423.5 65.0 %all-gather.28.cloned.1.call-done = bf16[2048,1536]{1,0:T(8,128)(2,1)} async-done(((bf16[256,1536]{1,0:T(8,128)(2,1)}), bf16[2048,1536]{1,0:T(8,128)(2,1)}) %all-gather.28.cloned.1.call-update) | async-done | bytes 6291472 | tf_op jit(solution)/shard_map/all_gather | solution.py:184
  488.5 23.8 all-gather.26.cloned.1.call-done
  512.3 8.5 fusion.93
  520.8 91.8 %all-gather.30.cloned.1.call-done = bf16[2048,1536]{1,0:T(8,128)(2,1)} async-done(((bf16[256,1536]{1,0:T(8,128)(2,1)}), bf16[2048,1536]{1,0:T(8,128)(2,1)}) %all-gather.30.cloned.1.call-update) | async-done | bytes 6291472 | tf_op jit(solution)/shard_map/all_gather | solution.py:185
  612.6 8.5 fusion.94
  621.2 15.3 all-gather.34.cloned.1.call-done
  636.5 101.0 %all-gather.32.cloned.1.call-done = bf16[1536,2048]{1,0:T(8,128)(2,1)} async-done(((bf16[1536,256]{1,0:T(8,128)(2,1)}), bf16[1536,2048]{1,0:T(8,128)(2,1)}) %all-gather.32.cloned.1.call-update) | async-done | bytes 6291472 | tf_op jit(solution)/shard_map/all_gather | solution.py:186
  737.5 12.0 multiply_convert_fusion
  749.5 6.7 fusion.96
  761.5 8.9 fusion.95
  784.0 9.8 slice.567
  793.8 9.9 slice.574
  803.7 9.9 slice.565
  816.1 35.7 %reduce-scatter.14.cloned.1.call-done = f32[128,2048]{1,0:T(8,128)} async-done(((f32[512,2048]{1,0:T(8,128)}), f32[128,2048]{1,0:T(8,128)}) %reduce-scatter.14.cloned.1.call-update) | async-done | bytes 1048592 | tf_op jit(solution)/shard_map/reduce_scatter | solution.py:193
  855.2 9.9 fusion.26
  871.9 9.9 slice.569
  881.7 9.8 slice.571
  963.1 9.9 slice.619
  1053.6 5.7 all-gather.4
  1065.0 10.7 rev.9
  1075.8 10.8 rev.8
  1118.0 5.6 multiply_reduce_fusion.4
  1132.1 7.9 fusion.100
  1140.4 7.9 fusion.101
  1149.9 7.9 fusion.102
  1159.2 8.7 fusion.73
  1169.0 8.8 fusion.75
  1188.3 8.8 fusion.77
  1197.8 7.5 fusion.97
  1205.3 7.6 fusion.38
  1212.9 39.8 %all-reduce.70 = (f32[2560]{0:T(1024)S(1)}, f32[2560]{0:T(1024)S(1)}, f32[2560]{0:T(1024)S(1)}, f32[2560]{0:T(1024)S(1)}, f32[2048]{0:T(1024)S(1)}, /*index=5*/f32[2048]{0:T(1024)S(1)}) all-reduce(f32[2560]{0:T(1024)S(1)} %get-tuple-element.157, ...), channel_id=10, replica_groups=mesh['seq'=4,'batch'=8] {'seq','batch'}, use_global_device_ids=true, to_apply=%region_21.22.clone | all-reduce | flops 14336 | bytes 114688
  1259.0 132.8 %reduce-scatter.24.cloned.1.call-done = f32[80,256]{1,0:T(8,128)} async-done(((f32[2560,256]{1,0:T(8,128)}), f32[80,256]{1,0:T(8,128)}) %reduce-scatter.24.cloned.1.call-update) | async-done | bytes 81936 | tf_op jit(solution)/shard_map/reduce_scatter | solution.py:320
  1391.8 139.0 %reduce-scatter.26.cloned.1.call-done = f32[80,256]{1,0:T(8,128)} async-done(((f32[2560,256]{1,0:T(8,128)}), f32[80,256]{1,0:T(8,128)}) %reduce-scatter.26.cloned.1.call-update) | async-done | bytes 81936 | tf_op jit(solution)/shard_map/reduce_scatter | solution.py:321
  1530.8 216.8 %reduce-scatter.28.cloned.1.call-done = f32[256,1536]{1,0:T(8,128)} async-done(((f32[2048,1536]{1,0:T(8,128)}), f32[256,1536]{1,0:T(8,128)}) %reduce-scatter.28.cloned.1.call-update) | async-done | bytes 1572880 | tf_op jit(solution)/shard_map/reduce_scatter | solution.py:211
  1747.6 211.0 %reduce-scatter.30.cloned.1.call-done = f32[256,1536]{1,0:T(8,128)} async-done(((f32[2048,1536]{1,0:T(8,128)}), f32[256,1536]{1,0:T(8,128)}) %reduce-scatter.30.cloned.1.call-update) | async-done | bytes 1572880 | tf_op jit(solution)/shard_map/reduce_scatter | solution.py:217
  1958.6 211.3 %reduce-scatter.32.cloned.1.call-done = f32[1536,256]{1,0:T(8,128)} async-done(((f32[1536,2048]{1,0:T(8,128)}), f32[1536,256]{1,0:T(8,128)}) %reduce-scatter.32.cloned.1.call-update) | async-done | bytes 1572880 | tf_op jit(solution)/shard_map/reduce_scatter | solution.py:223
  2169.9 446.1 %reduce-scatter.22.cloned.1.call-done = f32[80,2048]{1,0:T(8,128)} async-done(((f32[2560,2048]{1,0:T(8,128)}), f32[80,2048]{1,0:T(8,128)}) %reduce-scatter.22.cloned.1.call-update) | async-done | bytes 655376 | tf_op jit(solution)/shard_map/reduce_scatter | solution.py:319
  2616.0 447.3 %reduce-scatter.20.cloned.1.call-done = f32[64,2560]{1,0:T(8,128)} async-done(((f32[2048,2560]{1,0:T(8,128)}), f32[64,2560]{1,0:T(8,128)}) %reduce-scatter.20.cloned.1.call-update) | async-done | bytes 655376 | tf_op jit(solution)/shard_map/reduce_scatter | solution.py:318
  3063.3 447.5 %reduce-scatter.18.cloned.1.call-done = f32[64,2560]{1,0:T(8,128)} async-done(((f32[2048,2560]{1,0:T(8,128)}), f32[64,2560]{1,0:T(8,128)}) %reduce-scatter.18.cloned.1.call-update) | async-done | bytes 655376 | tf_op jit(solution)/shard_map/reduce_scatter | solution.py:317
  (565 shorter events, 455.5 us)
Async XLA Ops:
  7.3 48.1 %copy-start = (bf16[1,128,2048]{2,1,0:T(8,128)(2,1)S(1)}, bf16[1,128,2048]{2,1,0:T(8,128)(2,1)}, u32[]{:S(2)}) copy-start(bf16[1,128,2048]{2,1,0:T(8,128)(2,1)} %param.22) | copy-start | bytes 1572868
  7.3 48.3 %copy-start.92 = (bf16[4,80]{1,0:T(4,128)(2,1)S(1)}, bf16[4,80]{1,0:T(4,128)(2,1)}, u32[]{:S(2)}) copy-start(bf16[4,80]{1,0:T(4,128)(2,1)} %param.30) | copy-start | bytes 1924
  7.3 111.0 %all-gather.18.cloned.1.call-start = ((), (), s32[]{:S(2)}) async-start(), calls=%async_computation.12 | async-start | bytes 10813440 | tf_op jit(solution)/shard_map/all_gather | solution.py:114
  8.0 148.9 %all-gather.20.cloned.1.call-start = ((), (), s32[]{:S(2)}) async-start(), calls=%async_computation.13 | async-start | bytes 1351680 | tf_op jit(solution)/shard_map/all_gather | solution.py:117
  8.8 204.4 %all-gather.22.cloned.1.call-start = ((), (), s32[]{:S(2)}) async-start(), calls=%async_computation.14 | async-start | bytes 1351680 | tf_op jit(solution)/shard_map/all_gather | solution.py:118
  9.5 393.3 %all-gather.16.cloned.1.call-start = ((), (), s32[]{:S(2)}) async-start(), calls=%async_computation.11 | async-start | bytes 10813440 | tf_op jit(solution)/shard_map/all_gather | solution.py:115
  10.1 402.0 %all-gather.24.cloned.1.call-start = ((), (), s32[]{:S(2)}) async-start(), calls=%async_computation.15 | async-start | bytes 10813440 | tf_op jit(solution)/shard_map/all_gather | solution.py:116
  10.7 477.8 %all-gather.28.cloned.1.call-start = ((), (), s32[]{:S(2)}) async-start(), calls=%async_computation.17 | async-start | bytes 7077888 | tf_op jit(solution)/shard_map/all_gather | solution.py:184
  11.2 501.1 %all-gather.26.cloned.1.call-start = ((), (), s32[]{:S(2)}) async-start(), calls=%async_computation.16 | async-start | bytes 2621440 | tf_op jit(solution)/shard_map/all_gather | solution.py:188
  55.3 68.5 %copy-start.88 = (bf16[2560]{0:T(1024)(128)(2,1)}, bf16[2560]{0:T(1024)(128)(2,1)S(1)}, u32[]{:S(2)}) copy-start(bf16[2560]{0:T(1024)(128)(2,1)S(1)} %get-tuple-element.188) | copy-start | bytes 15364
  55.3 68.5 %copy-start.39 = (f32[2048]{0:T(1024)}, f32[2048]{0:T(1024)S(1)}, u32[]{:S(2)}) copy-start(f32[2048]{0:T(1024)S(1)} %convert_element_type.96) | copy-start | bytes 24580
  55.6 68.3 %copy-start.67 = (f32[128]{0:T(128)}, f32[128]{0:T(128)S(1)}, u32[]{:S(2)}) copy-start(f32[128]{0:T(128)S(1)} %add_rsqrt_fusion.1) | copy-start | bytes 1540
  117.5 104.2 %copy-start.46 = (f32[2560]{0:T(1024)}, f32[2560]{0:T(1024)S(1)}, u32[]{:S(2)}) copy-start(f32[2560]{0:T(1024)S(1)} %get-tuple-element.158) | copy-start | bytes 30724
  117.5 104.2 %copy-start.48 = (f32[2560]{0:T(1024)}, f32[2560]{0:T(1024)S(1)}, u32[]{:S(2)}) copy-start(f32[2560]{0:T(1024)S(1)} %get-tuple-element.159) | copy-start | bytes 30724
  117.6 104.2 %copy-start.50 = (f32[2560]{0:T(1024)}, f32[2560]{0:T(1024)S(1)}, u32[]{:S(2)}) copy-start(f32[2560]{0:T(1024)S(1)} %get-tuple-element.160) | copy-start | bytes 30724
  117.6 104.2 %copy-start.52 = (f32[2560]{0:T(1024)}, f32[2560]{0:T(1024)S(1)}, u32[]{:S(2)}) copy-start(f32[2560]{0:T(1024)S(1)} %get-tuple-element.161) | copy-start | bytes 30724
  117.6 104.2 %copy-start.42 = (f32[2560]{0:T(1024)}, f32[2560]{0:T(1024)S(1)}, u32[]{:S(2)}) copy-start(f32[2560]{0:T(1024)S(1)} %fusion.62) | copy-start | bytes 30724
  123.9 8.8 collective-permute-start
  132.1 89.7 %copy-start.56 = (f32[2560]{0:T(1024)}, f32[2560]{0:T(1024)S(1)}, u32[]{:S(2)}) copy-start(f32[2560]{0:T(1024)S(1)} %convert_element_type.98) | copy-start | bytes 30724
  132.1 89.7 %copy-start.44 = (f32[2560]{0:T(1024)}, f32[2560]{0:T(1024)S(1)}, u32[]{:S(2)}) copy-start(f32[2560]{0:T(1024)S(1)} %convert_element_type.103) | copy-start | bytes 30724
  132.1 89.7 %copy-start.54 = (f32[2560]{0:T(1024)}, f32[2560]{0:T(1024)S(1)}, u32[]{:S(2)}) copy-start(f32[2560]{0:T(1024)S(1)} %convert_element_type.105) | copy-start | bytes 30724
  133.8 25.8 copy-start.3
  391.3 11.4 copy-start.40
  391.3 11.4 copy-start.68
  420.1 192.6 %all-gather.30.cloned.1.call-start = ((), (), s32[]{:S(2)}) async-start(), calls=%async_computation.18 | async-start | bytes 7077888 | tf_op jit(solution)/shard_map/all_gather | solution.py:185
  420.8 215.7 %all-gather.34.cloned.1.call-start = ((), (), s32[]{:S(2)}) async-start(), calls=%async_computation.21 | async-start | bytes 2621440 | tf_op jit(solution)/shard_map/all_gather | solution.py:202
  422.9 314.6 %all-gather.32.cloned.1.call-start = ((), (), s32[]{:S(2)}) async-start(), calls=%async_computation.19 | async-start | bytes 7077888 | tf_op jit(solution)/shard_map/all_gather | solution.py:186
  423.5 390.2 %reduce-scatter.16.cloned.1.call-start = ((), (), s32[]{:S(2)}) async-start(), calls=%async_computation.22 | async-start | bytes 5242880 | tf_op jit(solution)/shard_map/reduce_scatter | solution.py:209
  737.5 18.8 slice-start
  761.5 90.4 %reduce-scatter.14.cloned.1.call-start = ((), (), s32[]{:S(2)}) async-start(), calls=%async_computation.20 | async-start | bytes 5242880 | tf_op jit(solution)/shard_map/reduce_scatter | solution.py:193
  770.4 487.1 %reduce-scatter.34.cloned.1.call-start = ((), (), s32[]{:S(2)}) async-start(), calls=%async_computation.31 | async-start | bytes 1351680
  958.1 14.9 copy-start.80
  958.1 14.9 copy-start.81
  958.1 14.9 copy-start.65
  958.1 15.0 copy-start.78
  958.1 15.0 copy-start.79
  958.1 15.1 copy-start.66
  958.1 15.8 copy-start.60
  958.1 15.8 copy-start.61
  1125.3 266.6 %reduce-scatter.24.cloned.1.call-start = ((), (), s32[]{:S(2)}) async-start(), calls=%async_computation.26 | async-start | bytes 2703360 | tf_op jit(solution)/shard_map/reduce_scatter | solution.py:320
  1127.4 403.4 %reduce-scatter.26.cloned.1.call-start = ((), (), s32[]{:S(2)}) async-start(), calls=%async_computation.27 | async-start | bytes 2703360 | tf_op jit(solution)/shard_map/reduce_scatter | solution.py:321
  1130.5 617.1 %reduce-scatter.28.cloned.1.call-start = ((), (), s32[]{:S(2)}) async-start(), calls=%async_computation.28 | async-start | bytes 14155776 | tf_op jit(solution)/shard_map/reduce_scatter | solution.py:211
  1140.0 818.6 %reduce-scatter.30.cloned.1.call-start = ((), (), s32[]{:S(2)}) async-start(), calls=%async_computation.29 | async-start | bytes 14155776 | tf_op jit(solution)/shard_map/reduce_scatter | solution.py:217
  1148.3 1021.6 %reduce-scatter.32.cloned.1.call-start = ((), (), s32[]{:S(2)}) async-start(), calls=%async_computation.30 | async-start | bytes 14155776 | tf_op jit(solution)/shard_map/reduce_scatter | solution.py:223
  1157.8 1458.2 %reduce-scatter.22.cloned.1.call-start = ((), (), s32[]{:S(2)}) async-start(), calls=%async_computation.25 | async-start | bytes 21626880 | tf_op jit(solution)/shard_map/reduce_scatter | solution.py:319
  1168.0 1895.4 %reduce-scatter.20.cloned.1.call-start = ((), (), s32[]{:S(2)}) async-start(), calls=%async_computation.24 | async-start | bytes 21626880 | tf_op jit(solution)/shard_map/reduce_scatter | solution.py:318
  1177.8 2333.0 %reduce-scatter.18.cloned.1.call-start = ((), (), s32[]{:S(2)}) async-start(), calls=%async_computation.23 | async-start | bytes 21626880 | tf_op jit(solution)/shard_map/reduce_scatter | solution.py:317
  1178.8 5.7 collective-permute-start.1
  (80 other events, 406.1 us)
Sparse Core Ops, SparseCore 0:
  11.0 89.8 all-gather.17
  103.8 53.0 all-gather.19
  159.7 53.3 all-gather.21
  215.9 85.7 all-gather.15
  304.4 85.3 all-gather.23
  391.8 96.5 all-gather.27
  490.6 21.6 all-gather.25
  514.5 98.1 all-gather.29
  614.8 21.6 all-gather.33
  638.4 99.0 all-gather.31
  761.6 43.1 reduce-scatter.15
  807.3 44.5 reduce-scatter.13
  1125.4 127.5 reduce-scatter.33
  1255.7 136.0 reduce-scatter.23
  1394.6 136.1 reduce-scatter.25
  1535.2 212.3 reduce-scatter.27
  1752.1 206.4 reduce-scatter.29
  1963.1 206.8 reduce-scatter.31
  2172.9 443.0 reduce-scatter.21
  2618.8 444.4 reduce-scatter.19
  3066.3 444.4 reduce-scatter.17
where the time goes:
time: 3540 us; the launch traced here: 3520 us
  waiting for transfers between devices  2660 us (75%)
  local copies, waits for them, and re-layouts  371 us (10%)
  blocking collectives  165 us (5%)
  matrix products  162 us (5%)
  other arithmetic  127 us (4%)
    reduce_scatter x1, waiting for transfers between devices, on_device(): lax.psum_scatter(grad_input_full, ('seq', 'batch'), scatter_dimension=0,...  447 us
    reduce_scatter x1, waiting for transfers between devices, on_device(): lax.psum_scatter(grad_branch_full, ('seq', 'batch'), scatter_dimension=0,...  447 us
    reduce_scatter x1, waiting for transfers between devices, on_device(): lax.psum_scatter(grad_output_full, ('seq', 'batch'), scatter_dimension=0,...  446 us
    reduce_scatter x1, waiting for transfers between devices, on_device(): lax.psum_scatter(jnp.einsum('td,tf->df', all_rows, grad_pre, preferred_el...  217 us
    reduce_scatter x1, waiting for transfers between devices, on_device(): lax.psum_scatter(jnp.einsum('tf,td->fd', hidden, grad_all, preferred_elem...  211 us
    reduce_scatter x1, waiting for transfers between devices, on_device(): lax.psum_scatter(jnp.einsum('td,tf->df', all_rows, grad_lin, preferred_el...  211 us
    reduce_scatter x1, waiting for transfers between devices, on_device(): lax.psum_scatter(grad_inlet_full, ('seq', 'batch'), scatter_dimension=0,...  139 us
    slice x49, local copies, waits for them, and re-layouts, on_device(): lax.associative_scan(affine_join, (next_decays, grad_states), axis=0, rev...  134 us
  transfers between devices with their start and end apart: 23, of which 17 were waited for; matrix products, arithmetic and copies ran while one was open for 10% of the time, Pallas kernels for 0%

commit v1 on v0

v1 whole, which is shorter than its diff:
```python
import functools

import jax
import jax.numpy as jnp
from jax import lax
from jax.experimental import pallas as pl
from jax.experimental.pallas import tpu as pltpu
from jax.sharding import Mesh
from jax.sharding import PartitionSpec as P

HB = 256
EVERY = ("x", "core", "z", "y")
F32 = jnp.float32
BF16 = jnp.bfloat16

epsilon = 1e-06


def rotated(block, axis, distance):
    count = lax.axis_size(axis)
    return lax.ppermute(block, axis, [(i, (i + distance) % count) for i in range(count)])


def shifted(block, axis, distance):
    count = lax.axis_size(axis)
    route = [(i, i + distance) for i in range(count) if 0 <= i + distance < count]
    return lax.ppermute(block, axis, route)


def spread(block, axis, dim):
    count = lax.axis_size(axis)
    place = lax.axis_index(axis)
    if count == 2:
        other = rotated(block, axis, 1)
        low = place == 0
        return jnp.stack(
            [jnp.where(low, block, other), jnp.where(low, other, block)], axis=dim
        )
    shape = block.shape[:dim] + (count,) + block.shape[dim:]
    whole = jnp.zeros(shape, block.dtype)
    for distance in range(count):
        piece = block if distance == 0 else rotated(block, axis, distance)
        source = lax.rem(place - distance + count, count)
        whole = lax.dynamic_update_slice_in_dim(
            whole, jnp.expand_dims(piece, dim), source, dim
        )
    return whole


def pick(array, index, dim):
    return lax.dynamic_index_in_dim(array, index, dim, keepdims=False)


def collect(partial, axis, dim):
    count = lax.axis_size(axis)
    place = lax.axis_index(axis)
    if count == 2:
        got = rotated(pick(partial, 1 - place, dim).astype(BF16), axis, 1)
        return pick(partial, place, dim).astype(F32) + got.astype(F32)
    blocks = jnp.moveaxis(partial, dim, 0).astype(BF16)
    got = lax.all_to_all(blocks, axis, 0, 0)
    return jnp.sum(got.astype(F32), axis=0)


def pair_rows(block):
    return spread(block, "core", 0).reshape((2 * block.shape[0],) + block.shape[1:])


def pair_sum(partial):
    rows = partial.shape[0] // 2
    halves = partial.reshape(2, rows, partial.shape[1])
    core = lax.axis_index("core")
    return pick(halves, core, 0) + rotated(pick(halves, 1 - core, 0), "core", 1)


def swap_columns(block):
    rows, width = block.shape[0], block.shape[1] // 2
    halves = block.reshape(rows, 2, width)
    core = lax.axis_index("core")
    own = pick(halves, core, 1)
    other = rotated(pick(halves, 1 - core, 1), "core", 1)
    low = core == 0
    return jnp.stack([jnp.where(low, own, other), jnp.where(low, other, own)], axis=0)


def unswap_columns(rows_both):
    core = lax.axis_index("core")
    own = pick(rows_both, core, 0)
    other = rotated(pick(rows_both, 1 - core, 0), "core", 1)
    low = core == 0
    return jnp.concatenate([jnp.where(low, own, other), jnp.where(low, other, own)], axis=1)


def half_route():
    count = lax.axis_size("x")
    return [(s, (s % count) * 2 + s // count) for s in range(2 * count)]


def to_half(block):
    return lax.ppermute(block, ("x", "core"), half_route())


def from_half(block):
    return lax.ppermute(block, ("x", "core"), [(b, a) for a, b in half_route()])


def share_small(vector):
    count = lax.axis_size(EVERY)
    return lax.all_to_all(jnp.broadcast_to(vector[None], (count,) + vector.shape), EVERY, 0, 0)


def gelu_tanh(values):
    return jax.nn.gelu(values, approximate=True)


def rms_factor(values):
    return lax.rsqrt(jnp.mean(values * values, axis=-1, keepdims=True) + epsilon)


def norm_backward(grad_normed, scaled, factor, gain):
    weighted = grad_normed * gain
    inner_mean = jnp.mean(weighted * scaled, axis=-1, keepdims=True)
    return (factor * (weighted - scaled * inner_mean), jnp.sum(grad_normed * scaled, axis=0))


def scan_kernel(reverse, decay_ref, drive_ref, cumulative_ref, local_ref):
    decay, drive = decay_ref[...], drive_ref[...]
    rows, width = decay.shape
    step = 1
    while step < rows:
        ones, zeros = jnp.ones((step, width), F32), jnp.zeros((step, width), F32)
        if reverse:
            decay_before = jnp.concatenate([decay[step:], ones], axis=0)
            drive_before = jnp.concatenate([drive[step:], zeros], axis=0)
        else:
            decay_before = jnp.concatenate([ones, decay[: rows - step]], axis=0)
            drive_before = jnp.concatenate([zeros, drive[: rows - step]], axis=0)
        drive = drive + decay * drive_before
        decay = decay * decay_before
        step *= 2
    cumulative_ref[...] = decay
    local_ref[...] = drive


def scan(decay, drive, reverse):
    rows, width = decay.shape
    block = pl.BlockSpec((rows, HB), lambda i: (0, i))
    shape = jax.ShapeDtypeStruct((rows, width), F32)
    return pl.pallas_call(
        functools.partial(scan_kernel, reverse),
        grid=(width // HB,),
        in_specs=[block, block],
        out_specs=[block, block],
        out_shape=[shape, shape],
        compiler_params=pltpu.CompilerParams(vmem_limit_bytes=32 << 20),
        cost_estimate=pl.CostEstimate(
            flops=24 * rows * width, bytes_accessed=16 * rows * width, transcendentals=0
        ),
    )(decay, drive)


def head_product(values, weights):
    rows, width = values.shape
    heads = width // HB
    return jnp.einsum(
        "thi,hij->thj",
        values.reshape(rows, heads, HB),
        weights.reshape(heads, HB, HB),
        preferred_element_type=F32,
    ).reshape(rows, width)


def head_product_back(values, weights):
    rows, width = values.shape
    heads = width // HB
    return jnp.einsum(
        "thj,hij->thi",
        values.reshape(rows, heads, HB),
        weights.reshape(heads, HB, HB),
        preferred_element_type=F32,
    ).reshape(rows, width)


def head_outer(left, right):
    rows, width = left.shape
    heads = width // HB
    return jnp.einsum(
        "thi,thj->hij",
        left.reshape(rows, heads, HB),
        right.reshape(rows, heads, HB),
        preferred_element_type=F32,
    ).reshape(width, HB)


def dot(left, right):
    return jnp.dot(left, right, preferred_element_type=F32)


def dot_t(left, right):
    return lax.dot_general(left, right, (((1,), (1,)), ((), ())), preferred_element_type=F32)


def outer(left, right):
    return lax.dot_general(left, right, (((0,), (0,)), ((), ())), preferred_element_type=F32)


def gather_rows(block):
    rows, width = block.shape[1:]
    block = spread(block, "z", 1)
    block = spread(block, "y", 2)
    block = spread(block, "x", 0)
    return block.reshape(-1, width)


def gather_half(block):
    width = block.shape[1]
    block = spread(block, "z", 0)
    block = spread(block, "y", 1)
    block = spread(block, "x", 0)
    return block.reshape(-1, width)


def gather_feed(block):
    width = block.shape[1]
    block = spread(block, "z", 0)
    block = spread(block, "y", 1)
    return block.reshape(-1, width)


def sum_rows(left, right, rows):
    x_count, z_count, y_count = (lax.axis_size(a) for a in ("x", "z", "y"))
    width = right.shape[1]
    partial = outer(left, right).reshape(x_count, 2, z_count, y_count, rows, width)
    partial = collect(partial, "x", 0)
    partial = collect(partial, "y", 2)
    return collect(partial, "z", 1)


def sum_half(partial, rows):
    x_count, z_count, y_count = (lax.axis_size(a) for a in ("x", "z", "y"))
    width = partial.shape[1]
    partial = partial.reshape(x_count, z_count, y_count, rows, width)
    partial = collect(partial, "x", 0)
    partial = collect(partial, "y", 1)
    return from_half(collect(partial, "z", 0).astype(BF16)).astype(F32)


def sum_feed(left, right):
    z_count, y_count = lax.axis_size("z"), lax.axis_size("y")
    rows, width = left.shape[1] // (z_count * y_count), right.shape[1]
    place = lax.axis_index("y")
    columns = left.reshape(left.shape[0], z_count, y_count, rows)

    def part(which):
        return outer(pick(columns, which, 2).reshape(left.shape[0], z_count * rows), right)

    got = rotated(part(1 - place).astype(BF16), "y", 1)
    total = part(place) + got.astype(F32)
    return collect(total.reshape(z_count, rows, width), "z", 0)


def on_device(
    tokens,
    lengths,
    cotangent,
    input_proj,
    branch_proj,
    output_proj,
    recur_gate,
    inlet_gate,
    conv_kernel,
    conv_bias,
    recur_bias,
    inlet_bias,
    decay_param,
    mixer_gain,
    feed_gain,
    feed_gate,
    feed_up,
    feed_down,
):
    x_count, z_count, y_count = (lax.axis_size(a) for a in ("x", "z", "y"))
    x_place, core = lax.axis_index("x"), lax.axis_index("core")
    own_rows, model = tokens.shape[1:]
    channels = conv_kernel.shape[1]
    gain_width = mixer_gain.shape[0]
    first = (x_place * 2 + core) * own_rows
    positions = first + jnp.arange(own_rows, dtype=jnp.int32)
    validity = (positions < lengths[0]).astype(F32)[:, None]

    vectors = jnp.concatenate(
        [
            conv_kernel.reshape(-1),
            conv_bias,
            recur_bias,
            inlet_bias,
            decay_param,
            mixer_gain,
            feed_gain,
        ]
    )
    everyone = share_small(vectors)
    by_channel = everyone[:, : 8 * channels].reshape(-1, 8, channels)
    gains = everyone[:, 8 * channels :].reshape(-1, 2, gain_width).transpose(1, 0, 2)
    gain_one, gain_two = gains.reshape(2, -1).astype(F32)
    half = by_channel.shape[0] // 2
    by_channel = lax.dynamic_slice_in_dim(by_channel, core * half, half, 0)
    by_channel = by_channel.transpose(1, 0, 2).reshape(8, -1).astype(F32)
    kernel_wide, bias_conv, bias_recur, bias_inlet, param_wide = (
        by_channel[:4],
        by_channel[4],
        by_channel[5],
        by_channel[6],
        by_channel[7],
    )

    input_full = gather_rows(swap_columns(input_proj))
    branch_full = gather_rows(swap_columns(branch_proj))
    gates_full = gather_half(to_half(jnp.concatenate([recur_gate, inlet_gate], axis=1)))
    recur_full, inlet_full = gates_full[:, :HB], gates_full[:, HB:]
    output_full = gather_half(to_half(output_proj))
    gate_local = gather_feed(feed_gate)
    lin_local = gather_feed(feed_up)
    down_local = gather_feed(feed_down.T)

    grad_out = cotangent[0].astype(F32)
    grad_feed = (validity * grad_out).astype(BF16)
    everyones_rows = lambda block: spread(spread(block, "x", 0), "core", 1).reshape(-1, model)
    grad_all = everyones_rows(grad_feed)

    channel_rate = jax.nn.softplus(param_wide)
    token_rows = tokens[0].astype(F32)
    factor_one = rms_factor(token_rows)
    scaled_one = token_rows * factor_one
    normed = pair_rows((scaled_one * gain_one).astype(BF16))
    rows = normed.shape[0]
    branch = dot(normed, branch_full)
    inner_proj = dot(normed, input_full).astype(BF16)
    rim_rows = shifted(inner_proj[rows - 3 :], "x", 1)
    extended = jnp.concatenate([rim_rows, inner_proj], axis=0)
    extended_wide = extended.astype(F32)
    convolved = bias_conv + kernel_wide[0] * extended_wide[3 : 3 + rows]
    for offset in range(1, 4):
        convolved = convolved + kernel_wide[offset] * extended_wide[3 - offset : 3 - offset + rows]
    conv_low = convolved.astype(BF16)
    recurrence = jax.nn.sigmoid(head_product(conv_low, recur_full) + bias_recur)
    inlets = jax.nn.sigmoid(head_product(conv_low, inlet_full) + bias_inlet)
    log_decay = -8.0 * recurrence * channel_rate
    decays = jnp.exp(log_decay)
    scaling = jnp.sqrt(-jnp.expm1(2.0 * log_decay))
    conv_value = conv_low.astype(F32)
    cumulative, local_state = scan(decays, scaling * inlets * conv_value, False)
    state_in = jnp.zeros_like(local_state[0])
    for _ in range(x_count - 1):
        state_in = shifted(cumulative[rows - 1] * state_in + local_state[rows - 1], "x", 1)
    states = local_state + cumulative * state_in
    gate_values = gelu_tanh(branch)
    mixed_in = (gate_values * states).astype(BF16)
    mix = pair_sum(dot(mixed_in, output_full))
    middle = token_rows + validity * mix
    factor_two = rms_factor(middle)
    scaled_two = middle * factor_two
    normed_two = (scaled_two * gain_two).astype(BF16)

    all_rows = everyones_rows(normed_two)
    feed_pre = dot(all_rows, gate_local)
    feed_lin = dot(all_rows, lin_local)
    feed_act, gelu_pull = jax.vjp(gelu_tanh, feed_pre)
    hidden = (feed_act * feed_lin).astype(BF16)
    feed_grad_down = sum_feed(grad_all, hidden).T
    grad_hidden = dot(grad_all, down_local)
    grad_pre = gelu_pull(grad_hidden * feed_lin)[0].astype(BF16)
    grad_lin = (grad_hidden * feed_act).astype(BF16)
    grad_rows = dot_t(grad_pre, gate_local) + dot_t(grad_lin, lin_local)

    def owners_rows(partial):
        block = partial.reshape(x_count, 2, own_rows, model)
        block = pick(block, core, 1) + rotated(pick(block, 1 - core, 1), "core", 1)
        return collect(block, "x", 0)

    grad_normed_two = owners_rows(grad_rows)
    feed_out = owners_rows(dot_t(hidden, down_local))
    output = (middle + validity * feed_out).astype(BF16)[None]
    feed_grad_gate = sum_feed(all_rows, grad_pre)
    feed_grad_up = sum_feed(all_rows, grad_lin)

    grad_mid_norm, grad_gain_feed = norm_backward(grad_normed_two, scaled_two, factor_two, gain_two)
    grad_middle = grad_out + grad_mid_norm
    grad_mix = pair_rows((validity * grad_middle).astype(BF16))
    grad_output = sum_half(outer(mixed_in, grad_mix), output_proj.shape[0])
    grad_mixed = dot_t(grad_mix, output_full)
    grad_branch = jax.vjp(gelu_tanh, branch)[1](grad_mixed * states)[0].astype(BF16)
    grad_branch_proj = unswap_columns(sum_rows(normed, grad_branch, branch_proj.shape[0]))
    grad_states = grad_mixed * gate_values
    next_decays = jnp.concatenate([decays[1:], jnp.ones_like(decays[:1])], axis=0)
    back_cum, back_local = scan(next_decays, grad_states, True)
    incoming = jnp.zeros_like(back_local[0])
    for _ in range(x_count - 1):
        incoming = shifted(decays[0] * (back_cum[0] * incoming + back_local[0]), "x", -1)
    carried = back_local + back_cum * incoming
    previous = jnp.concatenate([state_in[None], states[:-1]], axis=0)
    drive_grad = carried * conv_value
    grad_log = carried * previous * decays - drive_grad * inlets * decays * decays / scaling
    grad_recur_pre = grad_log * (-8.0 * channel_rate) * recurrence * (1.0 - recurrence)
    grad_inlet_pre = drive_grad * scaling * inlets * (1.0 - inlets)
    grad_param = jnp.sum(grad_log * (-8.0 * recurrence), axis=0) * jax.nn.sigmoid(param_wide)
    rounded_recur = grad_recur_pre.astype(BF16)
    rounded_inlet = grad_inlet_pre.astype(BF16)
    grad_gates = sum_half(
        jnp.concatenate(
            [head_outer(conv_low, rounded_recur), head_outer(conv_low, rounded_inlet)], axis=1
        ),
        channels,
    )
    grad_conv = (
        carried * scaling * inlets
        + head_product_back(rounded_recur, recur_full)
        + head_product_back(rounded_inlet, inlet_full)
    )
    ahead = shifted(grad_conv[:3], "x", -1)
    extended_back = jnp.concatenate([grad_conv, ahead], axis=0)
    grad_inner = kernel_wide[0] * extended_back[0:rows]
    for offset in range(1, 4):
        grad_inner = grad_inner + kernel_wide[offset] * extended_back[offset : offset + rows]
    grad_inner = grad_inner.astype(BF16)
    grad_input_proj = unswap_columns(sum_rows(normed, grad_inner, input_proj.shape[0]))
    grad_kernel = jnp.stack(
        [
            jnp.sum(grad_conv * extended_wide[3 - offset : 3 - offset + rows], axis=0)
            for offset in range(4)
        ],
        axis=0,
    )
    grad_normed = pair_sum(dot_t(grad_inner, input_full) + dot_t(grad_branch, branch_full))
    grad_token_norm, grad_gain_mixer = norm_backward(grad_normed, scaled_one, factor_one, gain_one)
    grad_tokens = (grad_middle + grad_token_norm)[None]

    channel_sums = jnp.concatenate(
        [
            grad_kernel,
            jnp.stack(
                [
                    jnp.sum(grad_conv, axis=0),
                    jnp.sum(grad_recur_pre, axis=0),
                    jnp.sum(grad_inlet_pre, axis=0),
                    grad_param,
                ]
            ),
        ],
        axis=0,
    )
    channel_sums = channel_sums.reshape(8, half, channels).transpose(1, 0, 2)
    everyones = lax.dynamic_update_slice_in_dim(
        jnp.zeros((2 * half, 8, channels), F32), channel_sums, core * half, 0
    ).reshape(2 * half, 8 * channels)
    gain_sums = jnp.stack([grad_gain_mixer, grad_gain_feed]).reshape(2, 2 * half, gain_width)
    everyones = jnp.concatenate(
        [everyones, gain_sums.transpose(1, 0, 2).reshape(2 * half, 2 * gain_width)], axis=1
    )
    sums = jnp.sum(lax.all_to_all(everyones, EVERY, 0, 0), axis=0)
    by_channel = sums[: 8 * channels].reshape(8, channels)
    by_gain = sums[8 * channels :].reshape(2, gain_width)
    return (
        output,
        grad_tokens,
        grad_input_proj,
        grad_branch_proj,
        grad_output,
        grad_gates[:, :HB],
        grad_gates[:, HB:],
        by_channel[:4],
        by_channel[4],
        by_channel[5],
        by_channel[6],
        by_channel[7],
        by_gain[0],
        by_gain[1],
        feed_grad_gate,
        feed_grad_up,
        feed_grad_down,
    )


def solution(mesh):
    seq, batch = mesh.shape["seq"], mesh.shape["batch"]
    fine = Mesh(mesh.devices.reshape(seq // 2, 2, batch // 2, 2), EVERY)
    sequences, places = ("z", "y"), ("x", "core")
    rows = P(sequences, places, None)
    spread_rows, spread_columns, spread_all = P(EVERY, None), P(None, EVERY), P(EVERY)
    feed = P(sequences, places)
    feed_back = P(places, sequences)
    in_specs = (
        (rows, P(sequences), rows)
        + (spread_rows,) * 5
        + (spread_columns,)
        + (spread_all,) * 6
        + (feed, feed, feed_back)
    )
    out_specs = (
        (rows, rows)
        + (spread_rows,) * 5
        + (spread_columns,)
        + (spread_all,) * 6
        + (feed, feed, feed_back)
    )
    return jax.shard_map(
        on_device, mesh=fine, in_specs=in_specs, out_specs=out_specs, check_vma=False
    )
```

time: 3540 us -> 1210 us (0.34)
  waiting for transfers between devices: 2660 us -> 685 us
  local copies, waits for them, and re-layouts: 371 us -> 145 us
  blocking collectives: 165 us -> 0 us
  starting transfers between devices: 11.4 us -> 138 us
  matrix products: 162 us -> 100 us
    reduce_scatter x10 -> x0, waiting for transfers between devices: 2290 us -> none  [the longest x1 447 us: on_device(): lax.psum_scatter(grad_input_full, ('seq', 'batch'), scatter_dimension=0,...]
    ppermute x2 -> x67, waiting for transfers between devices: 3.31 us -> 636 us  [the longest x59 633 us: rotated(): lax.ppermute(block, axis, [(i, (i + distance) % count) for i in range(cou...]
    all_gather x10 -> x0, waiting for transfers between devices: 369 us -> none  [the longest x1 101 us: on_device(): lax.all_gather(feed_down, 'batch', axis=1, tiled=True)]
    slice x96 -> x11, local copies, waits for them, and re-layouts: 211 us -> 3.95 us  [the longest x1 1.14 us: on_device(): recur_full, inlet_full = (gates_full[:, :HB], gates_full[:, HB:])]
    pad x48 -> x0, local copies, waits for them, and re-layouts: 90.3 us -> none  [the longest x24 45.2 us: on_device(): lax.associative_scan(affine_join, (next_decays, grad_states), axis=0, rev...]
    all_gather x5 -> x0, blocking collectives: 83 us -> none  [the longest x1 61.7 us: on_device(): lax.all_gather(conv_kernel, ('seq', 'batch'), axis=1, tiled=True)]
    unnamed x2 -> x0, blocking collectives: 82.3 us -> none
    ppermute x2 -> x67, starting transfers between devices: 10 us -> 84.7 us  [the longest x59 59.6 us: rotated(): lax.ppermute(block, axis, [(i, (i + distance) % count) for i in range(cou...]
  transfers between devices with their start and end apart: 23 -> 76, of which waited for: 17 -> 40; matrix products, arithmetic and copies ran while one was open for 10% -> 26% of each run, Pallas kernels for 0% -> 0%
where the time goes in v1:
time: 1210 us; the launch traced here: 1200 us
  waiting for transfers between devices  685 us (57%)
  local copies, waits for them, and re-layouts  145 us (12%)
  starting transfers between devices  138 us (11%)
  other arithmetic  123 us (10%)
  matrix products  100 us (8%)
    ppermute x59, waiting for transfers between devices, rotated(): lax.ppermute(block, axis, [(i, (i + distance) % count) for i in range(cou...  633 us
    ppermute x59, starting transfers between devices, rotated(): lax.ppermute(block, axis, [(i, (i + distance) % count) for i in range(cou...  59.6 us
    another operation x34, other arithmetic, spread(): jnp.stack([jnp.where(low, block, other), jnp.where(low, other, block)], a...  41.2 us
    dot_general x9, matrix products, outer(): lax.dot_general(left, right, (((0,), (0,)), ((), ())), preferred_element_...  38.2 us
    all_to_all x1, waiting for transfers between devices, share_small(): lax.all_to_all(jnp.broadcast_to(vector[None], (count,) + vector.shape), E...  37.5 us
    dynamic_slice x7, local copies, waits for them, and re-layouts, pick(): return lax.dynamic_index_in_dim(array, index, dim, keepdims=False)  36 us
    all_to_all x7, starting transfers between devices, collect(): got = lax.all_to_all(blocks, axis, 0, 0)  30.8 us
    unnamed x235, local copies, waits for them, and re-layouts  27.2 us
  transfers between devices with their start and end apart: 76, of which 40 were waited for; matrix products, arithmetic and copies ran while one was open for 26% of the time, Pallas kernels for 0%

profile of v1, /device:TPU:1, one launch (start us, length us, event | category | flops | bytes accessed | tf_op | source)
XLA Modules:
  0.0 1199.1 jit_solution(13728580657684883954)
XLA Ops:
  38.9 37.5 %all-to-all-done = bf16[32,2,384]{2,1,0:T(2,128)(2,1)S(1)} async-done(((bf16[32,2,384]{2,1,0:T(2,128)(2,1)}), bf16[32,2,384]{2,1,0:T(2,128)(2,1)S(1)}, u32[]{:S(2)}, u32[]{:S(2)}) %all-to-all-start) | async-done | bytes 49184 | tf_op jit(solution)/shard_map/all_to_all | solution.py:109
  82.7 5.2 collective-permute-done.8
  88.0 5.2 collective-permute-done.9
  99.9 10.9 collective-permute-done.2
  110.9 16.1 %collective-permute-done.3 = bf16[2,64,1280]{2,1,0:T(8,128)(2,1)S(1)} collective-permute-done((bf16[2,64,1280]{2,1,0:T(8,128)(2,1)S(1)}, bf16[2,64,1280]{2,1,0:T(8,128)(2,1)S(1)}, u32[]{:S(2)}, u32[]{:S(2)}) %collective-permute-start.3) | collective-permute-done | bytes 327712 | tf_op jit(solution)/shard_map/ppermute | solution.py:21
  129.3 6.6 collective-permute-done.4
  135.9 10.3 collective-permute-done.14
  146.2 16.3 %collective-permute-done.15 = bf16[2,64,1280]{2,1,0:T(8,128)(2,1)S(1)} collective-permute-done((bf16[2,64,1280]{2,1,0:T(8,128)(2,1)S(1)}, bf16[2,64,1280]{2,1,0:T(8,128)(2,1)S(1)}, u32[]{:S(2)}, u32[]{:S(2)}) %collective-permute-start.15) | collective-permute-done | bytes 327712 | tf_op jit(solution)/shard_map/ppermute | solution.py:21
  162.6 8.8 collective-permute-done.11
  173.6 5.7 collective-permute-done.16
  181.3 23.3 %collective-permute-done.22 = bf16[80,2048]{1,0:T(8,128)(2,1)S(1)} collective-permute-done((bf16[80,2048]{1,0:T(8,128)(2,1)S(1)}, bf16[80,2048]{1,0:T(8,128)(2,1)S(1)}, u32[]{:S(2)}, u32[]{:S(2)}) %collective-permute-start.22) | collective-permute-done | bytes 327712 | tf_op jit(solution)/shard_map/ppermute | solution.py:21
  206.6 14.5 %collective-permute-done.23 = bf16[80,2048]{1,0:T(8,128)(2,1)S(1)} collective-permute-done((bf16[80,2048]{1,0:T(8,128)(2,1)S(1)}, bf16[80,2048]{1,0:T(8,128)(2,1)S(1)}, u32[]{:S(2)}, u32[]{:S(2)}) %collective-permute-start.23) | collective-permute-done | bytes 327712 | tf_op jit(solution)/shard_map/ppermute | solution.py:21
  222.2 6.2 collective-permute-done.24
  239.2 28.5 %collective-permute-done.39 = bf16[256,1536]{1,0:T(8,128)(2,1)S(1)} collective-permute-done((bf16[256,1536]{1,0:T(8,128)(2,1)S(1)}, bf16[256,1536]{1,0:T(8,128)(2,1)S(1)}, u32[]{:S(2)}, u32[]{:S(2)}) %collective-permute-start.39) | collective-permute-done | bytes 786464 | tf_op jit(solution)/shard_map/ppermute | solution.py:21
  269.7 9.7 collective-permute-done.30
  280.6 51.9 %collective-permute-done.31 = bf16[256,1536]{1,0:T(8,128)(2,1)S(1)} collective-permute-done((bf16[256,1536]{1,0:T(8,128)(2,1)S(1)}, bf16[256,1536]{1,0:T(8,128)(2,1)S(1)}, u32[]{:S(2)}, u32[]{:S(2)}) %collective-permute-start.31) | collective-permute-done | bytes 786464 | tf_op jit(solution)/shard_map/ppermute | solution.py:21
  343.4 19.7 %collective-permute-done.25 = bf16[4,80,2048]{2,1,0:T(8,128)(2,1)S(1)} collective-permute-done((bf16[4,80,2048]{2,1,0:T(8,128)(2,1)S(1)}, bf16[4,80,2048]{2,1,0:T(8,128)(2,1)S(1)}, u32[]{:S(2)}, u32[]{:S(2)}) %collective-permute-start.25) | collective-permute-done | bytes 1310752 | tf_op jit(solution)/shard_map/ppermute | solution.py:21
  365.8 64.7 %collective-permute-done.37 = bf16[4,256,1536]{2,1,0:T(8,128)(2,1)S(1)} collective-permute-done((bf16[4,256,1536]{2,1,0:T(8,128)(2,1)S(1)}, bf16[4,256,1536]{2,1,0:T(8,128)(2,1)S(1)}, u32[]{:S(2)}, u32[]{:S(2)}) %collective-permute-start.37) | collective-permute-done | bytes 3145760 | tf_op jit(solution)/shard_map/ppermute | solution.py:21
  437.7 60.3 %collective-permute-done.41 = bf16[4,256,1536]{2,1,0:T(8,128)(2,1)} collective-permute-done((bf16[4,256,1536]{2,1,0:T(8,128)(2,1)S(1)}, bf16[4,256,1536]{2,1,0:T(8,128)(2,1)}, u32[]{:S(2)}, u32[]{:S(2)}) %collective-permute-start.41) | collective-permute-done | bytes 3145760 | tf_op jit(solution)/shard_map/ppermute | solution.py:21
  558.9 6.4 collective-permute-done.33
  572.1 10.1 collective-permute-done.44
  587.1 6.3 collective-permute-done.28
  608.6 5.6 fusion.87
  614.1 7.6 fusion.6
  626.8 5.3 convolution_add_fusion
  660.9 9.1 collective-permute-done.43
  674.7 6.4 constant_dynamic-slice_fusion
  681.1 5.8 copy.153
  686.9 5.2 convolution_convert_fusion
  695.8 5.5 fusion.65
  751.8 6.0 copy.152
  764.3 20.3 %all-to-all-start.5 = ((f32[32,1,768]{2,1,0:T(1,128)}), f32[32,1,768]{2,1,0:T(1,128)S(1)}, u32[]{:S(2)}, u32[]{:S(2)}) async-start(f32[32,1,768]{2,1,0:T(1,128)} %copy.148), calls=%async_computation.5 | async-start | bytes 196608 | tf_op jit(solution)/shard_map/all_to_all | solution.py:460
  786.6 5.5 all-to-all-done.5
  795.6 5.8 add_convert_fusion
  805.5 5.1 all-to-all-start.8
  813.9 6.4 constant_dynamic-slice_fusion.2
  820.4 5.8 copy.150
  826.2 5.3 convolution_convert_fusion.1
  836.4 63.8 %collective-permute-done.65 = bf16[1024,1536]{1,0:T(8,128)(2,1)} collective-permute-done((bf16[1024,1536]{1,0:T(8,128)(2,1)}, bf16[1024,1536]{1,0:T(8,128)(2,1)}, u32[]{:S(2)}, u32[]{:S(2)}) %collective-permute-start.65) | collective-permute-done | bytes 3145760 | tf_op jit(solution)/shard_map/ppermute | solution.py:21
  900.2 6.2 add_convert_fusion.1
  925.4 58.6 %collective-permute-done.64 = bf16[1024,1536]{1,0:T(8,128)(2,1)} collective-permute-done((bf16[1024,1536]{1,0:T(8,128)(2,1)}, bf16[1024,1536]{1,0:T(8,128)(2,1)}, u32[]{:S(2)}, u32[]{:S(2)}) %collective-permute-start.64) | collective-permute-done | bytes 3145760 | tf_op jit(solution)/shard_map/ppermute | solution.py:21
  984.0 6.2 add_convert_fusion.2
  1003.8 7.3 bitcast_add_fusion
  1017.9 39.6 %collective-permute-done.55 = bf16[2,4,2,64,1280]{4,3,2,1,0:T(8,128)(2,1)} collective-permute-done((bf16[2,4,2,64,1280]{4,3,2,1,0:T(8,128)(2,1)}, bf16[2,4,2,64,1280]{4,3,2,1,0:T(8,128)(2,1)}, u32[]{:S(2)}, u32[]{:S(2)}) %collective-permute-start.55) | collective-permute-done | bytes 2621472 | tf_op jit(solution)/shard_map/ppermute | solution.py:21
  1071.6 42.1 %collective-permute-done.52 = bf16[2,4,2,64,1280]{4,3,2,1,0:T(8,128)(2,1)} collective-permute-done((bf16[2,4,2,64,1280]{4,3,2,1,0:T(8,128)(2,1)}, bf16[2,4,2,64,1280]{4,3,2,1,0:T(8,128)(2,1)}, u32[]{:S(2)}, u32[]{:S(2)}) %collective-permute-start.52) | collective-permute-done | bytes 2621472 | tf_op jit(solution)/shard_map/ppermute | solution.py:21
  1113.7 6.2 bitcast_add_fusion.2
  1128.4 24.8 %collective-permute-done.53 = bf16[2,4,64,1280]{3,2,1,0:T(8,128)(2,1)S(1)} collective-permute-done((bf16[2,4,64,1280]{3,2,1,0:T(8,128)(2,1)S(1)}, bf16[2,4,64,1280]{3,2,1,0:T(8,128)(2,1)S(1)}, u32[]{:S(2)}, u32[]{:S(2)}) %collective-permute-start.53) | collective-permute-done | bytes 1310752 | tf_op jit(solution)/shard_map/ppermute | solution.py:21
  1164.4 8.3 collective-permute-start.63
  (590 shorter events, 397.5 us)
Async XLA Ops:
  0.7 227.9 %collective-permute-start.34 = (bf16[256,1536]{1,0:T(8,128)(2,1)}, bf16[256,1536]{1,0:T(8,128)(2,1)}, u32[]{:S(2)}, u32[]{:S(2)}) collective-permute-start(bf16[256,1536]{1,0:T(8,128)(2,1)} %param.34), channel_id=1, source_target_pairs={{0,2},{2,4},{4,6},{6,0},{1,3},{3,5},{5,7},{7,1},{8,10},{10,12},{12... | collective-permute-start | bytes 2359304 | tf_op jit(solution)/shard_map/ppermute | solution.py:21
  2.8 229.7 %collective-permute-start.35 = (bf16[256,1536]{1,0:T(8,128)(2,1)}, bf16[256,1536]{1,0:T(8,128)(2,1)}, u32[]{:S(2)}, u32[]{:S(2)}) collective-permute-start(bf16[256,1536]{1,0:T(8,128)(2,1)} %param.34), channel_id=1, source_target_pairs={{0,4},{2,6},{4,0},{6,2},{1,5},{3,7},{5,1},{7,3},{8,12},{10,14},{12... | collective-permute-start | bytes 2359304 | tf_op jit(solution)/shard_map/ppermute | solution.py:21
  5.2 229.2 %collective-permute-start.36 = (bf16[256,1536]{1,0:T(8,128)(2,1)}, bf16[256,1536]{1,0:T(8,128)(2,1)}, u32[]{:S(2)}, u32[]{:S(2)}) collective-permute-start(bf16[256,1536]{1,0:T(8,128)(2,1)} %param.34), channel_id=1, source_target_pairs={{0,6},{2,0},{4,2},{6,4},{1,7},{3,1},{5,3},{7,5},{8,14},{10,8},{12,... | collective-permute-start | bytes 2359304 | tf_op jit(solution)/shard_map/ppermute | solution.py:21
  6.2 93.4 %collective-permute-start.21 = (bf16[80,2048]{1,0:T(8,128)(2,1)}, bf16[80,2048]{1,0:T(8,128)(2,1)S(1)}, u32[]{:S(2)}, u32[]{:S(2)}) collective-permute-start(bf16[80,2048]{1,0:T(8,128)(2,1)} %param.23), channel_id=1, source_target_pairs={{0,0},{8,16},{16,8},{24,24},{1,1},{9,17},{17,9},{25,25},{2,2},{10,... | collective-permute-start | bytes 983048 | tf_op jit(solution)/shard_map/ppermute | solution.py:100
  17.7 58.7 %all-to-all-start = ((bf16[32,2,384]{2,1,0:T(2,128)(2,1)}), bf16[32,2,384]{2,1,0:T(2,128)(2,1)S(1)}, u32[]{:S(2)}, u32[]{:S(2)}) async-start(bf16[32,2,384]{2,1,0:T(2,128)(2,1)} %reshape.390), calls=%async_computation | async-start | bytes 98304 | tf_op jit(solution)/shard_map/all_to_all | solution.py:109
  21.5 16.4 %collective-permute-start.7 = (bf16[80,512]{1,0:T(8,128)(2,1)}, bf16[80,512]{1,0:T(8,128)(2,1)}, u32[]{:S(2)}, u32[]{:S(2)}) collective-permute-start(bf16[80,512]{1,0:T(8,128)(2,1)} %pad_maximum_fusion.22), channel_id=1, source_target_pairs={{0,0},{8,16},{16,8},{24,24},{1,1},{9,17},{17,9},{25,25},{2,2},{10,... | collective-permute-start | bytes 245768 | tf_op jit(solution)/shard_map/ppermute | solution.py:100
  37.9 42.5 %collective-permute-start.1 = (bf16[64,1280]{1,0:T(8,128)(2,1)S(1)}, bf16[64,1280]{1,0:T(8,128)(2,1)}, u32[]{:S(2)}, u32[]{:S(2)}) collective-permute-start(bf16[64,1280]{1,0:T(8,128)(2,1)S(1)} %bitcast.526), channel_id=1, source_target_pairs={{0,8},{8,0},{1,9},{9,1},{2,10},{10,2},{3,11},{11,3},{4,12},{12,4},... | collective-permute-start | bytes 491528 | tf_op jit(solution)/shard_map/ppermute | solution.py:21
  96.7 82.6 %collective-permute-start = (bf16[128,2048]{1,0:T(8,128)(2,1)S(1)}, bf16[128,2048]{1,0:T(8,128)(2,1)S(1)}, u32[]{:S(2)}, u32[]{:S(2)}) collective-permute-start(bf16[128,2048]{1,0:T(8,128)(2,1)S(1)} %fusion.47), channel_id=1, source_target_pairs={{0,8},{8,0},{1,9},{9,1},{2,10},{10,2},{3,11},{11,3},{4,12},{12,4},... | collective-permute-start | bytes 1572872 | tf_op jit(solution)/shard_map/ppermute | solution.py:21
  179.2 57.5 %collective-permute-start.38 = (bf16[256,1536]{1,0:T(8,128)(2,1)S(1)}, bf16[256,1536]{1,0:T(8,128)(2,1)S(1)}, u32[]{:S(2)}, u32[]{:S(2)}) collective-permute-start(bf16[256,1536]{1,0:T(8,128)(2,1)S(1)} %bitcast.512), channel_id=1, source_target_pairs={{0,2},{2,4},{4,6},{6,0},{1,3},{3,5},{5,7},{7,1},{8,10},{10,12},{12... | collective-permute-start | bytes 2359304 | tf_op jit(solution)/shard_map/ppermute | solution.py:21
  179.3 25.3 %collective-permute-start.22 = (bf16[80,2048]{1,0:T(8,128)(2,1)S(1)}, bf16[80,2048]{1,0:T(8,128)(2,1)S(1)}, u32[]{:S(2)}, u32[]{:S(2)}) collective-permute-start(bf16[80,2048]{1,0:T(8,128)(2,1)S(1)} %collective-permute-done.21), channel_id=1, source_target_pairs={{0,2},{2,4},{4,6},{6,0},{1,3},{3,5},{5,7},{7,1},{8,10},{10,12},{12... | collective-permute-start | bytes 983048 | tf_op jit(solution)/shard_map/ppermute | solution.py:21
  204.6 16.6 %collective-permute-start.23 = (bf16[80,2048]{1,0:T(8,128)(2,1)S(1)}, bf16[80,2048]{1,0:T(8,128)(2,1)S(1)}, u32[]{:S(2)}, u32[]{:S(2)}) collective-permute-start(bf16[80,2048]{1,0:T(8,128)(2,1)S(1)} %collective-permute-done.21), channel_id=1, source_target_pairs={{0,4},{2,6},{4,0},{6,2},{1,5},{3,7},{5,1},{7,3},{8,12},{10,14},{12... | collective-permute-start | bytes 983048 | tf_op jit(solution)/shard_map/ppermute | solution.py:21
  228.4 39.3 %collective-permute-start.39 = (bf16[256,1536]{1,0:T(8,128)(2,1)S(1)}, bf16[256,1536]{1,0:T(8,128)(2,1)S(1)}, u32[]{:S(2)}, u32[]{:S(2)}) collective-permute-start(bf16[256,1536]{1,0:T(8,128)(2,1)S(1)} %bitcast.513), channel_id=1, source_target_pairs={{0,4},{2,6},{4,0},{6,2},{1,5},{3,7},{5,1},{7,3},{8,12},{10,14},{12... | collective-permute-start | bytes 2359304 | tf_op jit(solution)/shard_map/ppermute | solution.py:21
  228.6 41.0 %collective-permute-start.40 = (bf16[256,1536]{1,0:T(8,128)(2,1)S(1)}, bf16[256,1536]{1,0:T(8,128)(2,1)S(1)}, u32[]{:S(2)}, u32[]{:S(2)}) collective-permute-start(bf16[256,1536]{1,0:T(8,128)(2,1)S(1)} %bitcast.514), channel_id=1, source_target_pairs={{0,6},{2,0},{4,2},{6,4},{1,7},{3,1},{5,3},{7,5},{8,14},{10,8},{12,... | collective-permute-start | bytes 2359304 | tf_op jit(solution)/shard_map/ppermute | solution.py:21
  232.6 46.9 %collective-permute-start.30 = (bf16[256,1536]{1,0:T(8,128)(2,1)S(1)}, bf16[256,1536]{1,0:T(8,128)(2,1)S(1)}, u32[]{:S(2)}, u32[]{:S(2)}) collective-permute-start(bf16[256,1536]{1,0:T(8,128)(2,1)S(1)} %copy-done.74), channel_id=1, source_target_pairs={{0,2},{2,4},{4,6},{6,0},{1,3},{3,5},{5,7},{7,1},{8,10},{10,12},{12... | collective-permute-start | bytes 2359304 | tf_op jit(solution)/shard_map/ppermute | solution.py:21
  234.3 98.2 %collective-permute-start.31 = (bf16[256,1536]{1,0:T(8,128)(2,1)S(1)}, bf16[256,1536]{1,0:T(8,128)(2,1)S(1)}, u32[]{:S(2)}, u32[]{:S(2)}) collective-permute-start(bf16[256,1536]{1,0:T(8,128)(2,1)S(1)} %copy-done.74), channel_id=1, source_target_pairs={{0,4},{2,6},{4,0},{6,2},{1,5},{3,7},{5,1},{7,3},{8,12},{10,14},{12... | collective-permute-start | bytes 2359304 | tf_op jit(solution)/shard_map/ppermute | solution.py:21
  236.7 99.1 %collective-permute-start.32 = (bf16[256,1536]{1,0:T(8,128)(2,1)S(1)}, bf16[256,1536]{1,0:T(8,128)(2,1)S(1)}, u32[]{:S(2)}, u32[]{:S(2)}) collective-permute-start(bf16[256,1536]{1,0:T(8,128)(2,1)S(1)} %copy-done.74), channel_id=1, source_target_pairs={{0,6},{2,0},{4,2},{6,4},{1,7},{3,1},{5,3},{7,5},{8,14},{10,8},{12,... | collective-permute-start | bytes 2359304 | tf_op jit(solution)/shard_map/ppermute | solution.py:21
  267.7 71.9 %collective-permute-start.5 = (bf16[2,4,64,1280]{3,2,1,0:T(8,128)(2,1)S(1)}, bf16[2,4,64,1280]{3,2,1,0:T(8,128)(2,1)S(1)}, u32[]{:S(2)}, u32[]{:S(2)}) collective-permute-start(bf16[2,4,64,1280]{3,2,1,0:T(8,128)(2,1)S(1)} %bitcast_dynamic-update-slice_fusion.23), channel_id=1, source_target_pairs={{0,1},{1,0},{2,3},{3,2},{4,5},{5,4},{6,7},{7,6},{8,9},{9,8},{10,11... | collective-permute-start | bytes 3932168 | tf_op jit(solution)/shard_map/ppermute | solution.py:21
  269.5 72.0 %collective-permute-start.17 = (bf16[2,4,64,1280]{3,2,1,0:T(8,128)(2,1)S(1)}, bf16[2,4,64,1280]{3,2,1,0:T(8,128)(2,1)S(1)}, u32[]{:S(2)}, u32[]{:S(2)}) collective-permute-start(bf16[2,4,64,1280]{3,2,1,0:T(8,128)(2,1)S(1)} %bitcast_dynamic-update-slice_fusion.12), channel_id=1, source_target_pairs={{0,1},{1,0},{2,3},{3,2},{4,5},{5,4},{6,7},{7,6},{8,9},{9,8},{10,11... | collective-permute-start | bytes 3932168 | tf_op jit(solution)/shard_map/ppermute | solution.py:21
  279.4 57.4 %collective-permute-start.12 = (bf16[4,2,80,512]{3,2,1,0:T(8,128)(2,1)S(1)}, bf16[4,2,80,512]{3,2,1,0:T(8,128)(2,1)S(1)}, u32[]{:S(2)}, u32[]{:S(2)}) collective-permute-start(bf16[4,2,80,512]{3,2,1,0:T(8,128)(2,1)S(1)} %pad_maximum_fusion.17), channel_id=1, source_target_pairs={{0,16},{16,0},{1,17},{17,1},{2,18},{18,2},{3,19},{19,3},{4,20},{20... | collective-permute-start | bytes 1966088 | tf_op jit(solution)/shard_map/ppermute | solution.py:21
  332.5 30.5 %collective-permute-start.25 = (bf16[4,80,2048]{2,1,0:T(8,128)(2,1)S(1)}, bf16[4,80,2048]{2,1,0:T(8,128)(2,1)S(1)}, u32[]{:S(2)}, u32[]{:S(2)}) collective-permute-start(bf16[4,80,2048]{2,1,0:T(8,128)(2,1)S(1)} %bitcast_dynamic-update-slice_fusion.19), channel_id=1, source_target_pairs={{0,1},{1,0},{2,3},{3,2},{4,5},{5,4},{6,7},{7,6},{8,9},{9,8},{10,11... | collective-permute-start | bytes 3932168 | tf_op jit(solution)/shard_map/ppermute | solution.py:21
  335.8 94.7 %collective-permute-start.37 = (bf16[4,256,1536]{2,1,0:T(8,128)(2,1)S(1)}, bf16[4,256,1536]{2,1,0:T(8,128)(2,1)S(1)}, u32[]{:S(2)}, u32[]{:S(2)}) collective-permute-start(bf16[4,256,1536]{2,1,0:T(8,128)(2,1)S(1)} %bitcast_dynamic-update-slice_fusion.4), channel_id=1, source_target_pairs={{0,1},{1,0},{2,3},{3,2},{4,5},{5,4},{6,7},{7,6},{8,9},{9,8},{10,11... | collective-permute-start | bytes 9437192 | tf_op jit(solution)/shard_map/ppermute | solution.py:21
  336.8 161.1 %collective-permute-start.41 = (bf16[4,256,1536]{2,1,0:T(8,128)(2,1)S(1)}, bf16[4,256,1536]{2,1,0:T(8,128)(2,1)}, u32[]{:S(2)}, u32[]{:S(2)}) collective-permute-start(bf16[4,256,1536]{2,1,0:T(8,128)(2,1)S(1)} %bitcast_dynamic-update-slice_fusion.1), channel_id=1, source_target_pairs={{0,1},{1,0},{2,3},{3,2},{4,5},{5,4},{6,7},{7,6},{8,9},{9,8},{10,11... | collective-permute-start | bytes 9437192 | tf_op jit(solution)/shard_map/ppermute | solution.py:21
  339.6 225.7 %collective-permute-start.33 = (bf16[4,256,1536]{2,1,0:T(8,128)(2,1)}, bf16[4,256,1536]{2,1,0:T(8,128)(2,1)}, u32[]{:S(2)}, u32[]{:S(2)}) collective-permute-start(bf16[4,256,1536]{2,1,0:T(8,128)(2,1)} %bitcast_dynamic-update-slice_fusion.8), channel_id=1, source_target_pairs={{0,1},{1,0},{2,3},{3,2},{4,5},{5,4},{6,7},{7,6},{8,9},{9,8},{10,11... | collective-permute-start | bytes 9437192 | tf_op jit(solution)/shard_map/ppermute | solution.py:21
  341.6 167.5 %collective-permute-start.6 = (bf16[2,4,2,64,1280]{4,3,2,1,0:T(8,128)(2,1)}, bf16[2,4,2,64,1280]{4,3,2,1,0:T(8,128)(2,1)}, u32[]{:S(2)}, u32[]{:S(2)}) collective-permute-start(bf16[2,4,2,64,1280]{4,3,2,1,0:T(8,128)(2,1)} %pad_maximum_fusion.6), channel_id=1, source_target_pairs={{0,16},{16,0},{1,17},{17,1},{2,18},{18,2},{3,19},{19,3},{4,20},{20... | collective-permute-start | bytes 7864328 | tf_op jit(solution)/shard_map/ppermute | solution.py:21
  363.1 139.8 %collective-permute-start.18 = (bf16[2,4,2,64,1280]{4,3,2,1,0:T(8,128)(2,1)}, bf16[2,4,2,64,1280]{4,3,2,1,0:T(8,128)(2,1)}, u32[]{:S(2)}, u32[]{:S(2)}) collective-permute-start(bf16[2,4,2,64,1280]{4,3,2,1,0:T(8,128)(2,1)} %pad_maximum_fusion.7), channel_id=1, source_target_pairs={{0,16},{16,0},{1,17},{17,1},{2,18},{18,2},{3,19},{19,3},{4,20},{20... | collective-permute-start | bytes 7864328 | tf_op jit(solution)/shard_map/ppermute | solution.py:21
  432.2 105.4 %collective-permute-start.26 = (bf16[4,2,80,2048]{3,2,1,0:T(8,128)(2,1)}, bf16[4,2,80,2048]{3,2,1,0:T(8,128)(2,1)}, u32[]{:S(2)}, u32[]{:S(2)}) collective-permute-start(bf16[4,2,80,2048]{3,2,1,0:T(8,128)(2,1)} %pad_maximum_fusion.8), channel_id=1, source_target_pairs={{0,16},{16,0},{1,17},{17,1},{2,18},{18,2},{3,19},{19,3},{4,20},{20... | collective-permute-start | bytes 7864328 | tf_op jit(solution)/shard_map/ppermute | solution.py:21
  545.5 23.1 %collective-permute-start.27 = (f32[128,2048]{1,0:T(8,128)}, f32[128,2048]{1,0:T(8,128)}, u32[]{:S(2)}, u32[]{:S(2)}) collective-permute-start(f32[128,2048]{1,0:T(8,128)} %dynamic-slice_bitcast_fusion.3), channel_id=1, source_target_pairs={{0,8},{8,0},{1,9},{9,1},{2,10},{10,2},{3,11},{11,3},{4,12},{12,4},... | collective-permute-start | bytes 3145736 | tf_op jit(solution)/shard_map/ppermute | solution.py:21
  570.6 22.8 %collective-permute-start.28 = (bf16[128,2048]{1,0:T(8,128)(2,1)S(1)}, bf16[128,2048]{1,0:T(8,128)(2,1)S(1)}, u32[]{:S(2)}, u32[]{:S(2)}) collective-permute-start(bf16[128,2048]{1,0:T(8,128)(2,1)S(1)} %multiply_convert_fusion.4), channel_id=1, source_target_pairs={{0,16},{16,0},{1,17},{17,1},{2,18},{18,2},{3,19},{19,3},{4,20},{20... | collective-permute-start | bytes 1572872 | tf_op jit(solution)/shard_map/ppermute | solution.py:21
  648.9 21.2 %collective-permute-start.43 = (bf16[128,2048]{1,0:T(8,128)(2,1)}, bf16[128,2048]{1,0:T(8,128)(2,1)}, u32[]{:S(2)}, u32[]{:S(2)}) collective-permute-start(bf16[128,2048]{1,0:T(8,128)(2,1)} %fusion.66), channel_id=1, source_target_pairs={{0,16},{16,0},{1,17},{17,1},{2,18},{18,2},{3,19},{19,3},{4,20},{20... | collective-permute-start | bytes 1572872 | tf_op jit(solution)/shard_map/ppermute | solution.py:21
  673.9 19.8 %collective-permute-start.48 = (bf16[128,2048]{1,0:T(8,128)(2,1)}, bf16[128,2048]{1,0:T(8,128)(2,1)}, u32[]{:S(2)}, u32[]{:S(2)}) collective-permute-start(bf16[128,2048]{1,0:T(8,128)(2,1)} %get-tuple-element.69), channel_id=1, source_target_pairs={{0,8},{8,0},{1,9},{9,1},{2,10},{10,2},{3,11},{11,3},{4,12},{12,4},... | collective-permute-start | bytes 1572872 | tf_op jit(solution)/shard_map/ppermute | solution.py:21
  692.1 103.4 %collective-permute-start.66 = (bf16[1024,1536]{1,0:T(8,128)(2,1)}, bf16[1024,1536]{1,0:T(8,128)(2,1)}, u32[]{:S(2)}, u32[]{:S(2)}) collective-permute-start(bf16[1024,1536]{1,0:T(8,128)(2,1)} %convolution_convert_fusion), channel_id=1, source_target_pairs={{0,1},{1,0},{2,3},{3,2},{4,5},{5,4},{6,7},{7,6},{8,9},{9,8},{10,11... | collective-permute-start | bytes 9437192 | tf_op jit(solution)/shard_map/ppermute | solution.py:21
  741.2 17.6 %collective-permute-start.61 = (bf16[4,2,80,512]{3,2,1,0:T(8,128)(2,1)}, bf16[4,2,80,512]{3,2,1,0:T(8,128)(2,1)}, u32[]{:S(2)}, u32[]{:S(2)}) collective-permute-start(bf16[4,2,80,512]{3,2,1,0:T(8,128)(2,1)} %fusion.59), channel_id=1, source_target_pairs={{0,16},{16,0},{1,17},{17,1},{2,18},{18,2},{3,19},{19,3},{4,20},{20... | collective-permute-start | bytes 1966088 | tf_op jit(solution)/shard_map/ppermute | solution.py:21
  760.3 24.3 %collective-permute-start.62 = (bf16[4,80,512]{2,1,0:T(8,128)(2,1)S(1)}, bf16[4,80,512]{2,1,0:T(8,128)(2,1)S(1)}, u32[]{:S(2)}, u32[]{:S(2)}) collective-permute-start(bf16[4,80,512]{2,1,0:T(8,128)(2,1)S(1)} %fusion.71), channel_id=1, source_target_pairs={{0,1},{1,0},{2,3},{3,2},{4,5},{5,4},{6,7},{7,6},{8,9},{9,8},{10,11... | collective-permute-start | bytes 983048 | tf_op jit(solution)/shard_map/ppermute | solution.py:21
  764.3 27.7 %all-to-all-start.5 = ((f32[32,1,768]{2,1,0:T(1,128)}), f32[32,1,768]{2,1,0:T(1,128)S(1)}, u32[]{:S(2)}, u32[]{:S(2)}) async-start(f32[32,1,768]{2,1,0:T(1,128)} %copy.148), calls=%async_computation.5 | async-start | bytes 196608 | tf_op jit(solution)/shard_map/all_to_all | solution.py:460
  805.5 100.9 %all-to-all-start.8 = ((bf16[4,256,1536]{2,1,0:T(8,128)(2,1)}), bf16[4,256,1536]{2,1,0:T(8,128)(2,1)}, u32[]{:S(2)}, u32[]{:S(2)}) async-start(bf16[4,256,1536]{2,1,0:T(8,128)(2,1)} %bitcast.511), calls=%async_computation.8 | async-start | bytes 6291456 | tf_op jit(solution)/shard_map/all_to_all | solution.py:61
  831.5 68.7 %collective-permute-start.65 = (bf16[1024,1536]{1,0:T(8,128)(2,1)}, bf16[1024,1536]{1,0:T(8,128)(2,1)}, u32[]{:S(2)}, u32[]{:S(2)}) collective-permute-start(bf16[1024,1536]{1,0:T(8,128)(2,1)} %convolution_convert_fusion.1), channel_id=1, source_target_pairs={{0,1},{1,0},{2,3},{3,2},{4,5},{5,4},{6,7},{7,6},{8,9},{9,8},{10,11... | collective-permute-start | bytes 9437192 | tf_op jit(solution)/shard_map/ppermute | solution.py:21
  906.4 83.8 %all-to-all-start.7 = ((bf16[4,256,1536]{2,1,0:T(8,128)(2,1)}), bf16[4,256,1536]{2,1,0:T(8,128)(2,1)}, u32[]{:S(2)}, u32[]{:S(2)}) async-start(bf16[4,256,1536]{2,1,0:T(8,128)(2,1)} %bitcast.510), calls=%async_computation.7 | async-start | bytes 6291456 | tf_op jit(solution)/shard_map/all_to_all | solution.py:61
  916.4 67.7 %collective-permute-start.64 = (bf16[1024,1536]{1,0:T(8,128)(2,1)}, bf16[1024,1536]{1,0:T(8,128)(2,1)}, u32[]{:S(2)}, u32[]{:S(2)}) collective-permute-start(bf16[1024,1536]{1,0:T(8,128)(2,1)} %convolution_convert_fusion.2), channel_id=1, source_target_pairs={{0,1},{1,0},{2,3},{3,2},{4,5},{5,4},{6,7},{7,6},{8,9},{9,8},{10,11... | collective-permute-start | bytes 9437192 | tf_op jit(solution)/shard_map/ppermute | solution.py:21
  924.9 78.8 %collective-permute-start.58 = (bf16[4,2,80,2048]{3,2,1,0:T(8,128)(2,1)}, bf16[4,2,80,2048]{3,2,1,0:T(8,128)(2,1)}, u32[]{:S(2)}, u32[]{:S(2)}) collective-permute-start(bf16[4,2,80,2048]{3,2,1,0:T(8,128)(2,1)} %fusion.9), channel_id=1, source_target_pairs={{0,16},{16,0},{1,17},{17,1},{2,18},{18,2},{3,19},{19,3},{4,20},{20... | collective-permute-start | bytes 7864328 | tf_op jit(solution)/shard_map/ppermute | solution.py:21
  990.2 75.0 %all-to-all-start.6 = ((bf16[4,256,1536]{2,1,0:T(8,128)(2,1)}), bf16[4,256,1536]{2,1,0:T(8,128)(2,1)}, u32[]{:S(2)}, u32[]{:S(2)}) async-start(bf16[4,256,1536]{2,1,0:T(8,128)(2,1)} %bitcast.509), calls=%async_computation.6 | async-start | bytes 6291456 | tf_op jit(solution)/shard_map/all_to_all | solution.py:61
  1002.1 55.4 %collective-permute-start.55 = (bf16[2,4,2,64,1280]{4,3,2,1,0:T(8,128)(2,1)}, bf16[2,4,2,64,1280]{4,3,2,1,0:T(8,128)(2,1)}, u32[]{:S(2)}, u32[]{:S(2)}) collective-permute-start(bf16[2,4,2,64,1280]{4,3,2,1,0:T(8,128)(2,1)} %fusion.8), channel_id=1, source_target_pairs={{0,16},{16,0},{1,17},{17,1},{2,18},{18,2},{3,19},{19,3},{4,20},{20... | collective-permute-start | bytes 7864328 | tf_op jit(solution)/shard_map/ppermute | solution.py:21
  1013.9 48.3 %collective-permute-start.59 = (bf16[4,80,2048]{2,1,0:T(8,128)(2,1)S(1)}, bf16[4,80,2048]{2,1,0:T(8,128)(2,1)S(1)}, u32[]{:S(2)}, u32[]{:S(2)}) collective-permute-start(bf16[4,80,2048]{2,1,0:T(8,128)(2,1)S(1)} %fusion.36), channel_id=1, source_target_pairs={{0,1},{1,0},{2,3},{3,2},{4,5},{5,4},{6,7},{7,6},{8,9},{9,8},{10,11... | collective-permute-start | bytes 3932168 | tf_op jit(solution)/shard_map/ppermute | solution.py:21
  1016.5 97.2 %collective-permute-start.52 = (bf16[2,4,2,64,1280]{4,3,2,1,0:T(8,128)(2,1)}, bf16[2,4,2,64,1280]{4,3,2,1,0:T(8,128)(2,1)}, u32[]{:S(2)}, u32[]{:S(2)}) collective-permute-start(bf16[2,4,2,64,1280]{4,3,2,1,0:T(8,128)(2,1)} %fusion.7), channel_id=1, source_target_pairs={{0,16},{16,0},{1,17},{17,1},{2,18},{18,2},{3,19},{19,3},{4,20},{20... | collective-permute-start | bytes 7864328 | tf_op jit(solution)/shard_map/ppermute | solution.py:21
  1065.2 56.2 %all-to-all-start.3 = ((bf16[4,80,2048]{2,1,0:T(8,128)(2,1)}), bf16[4,80,2048]{2,1,0:T(8,128)(2,1)S(1)}, u32[]{:S(2)}, u32[]{:S(2)}) async-start(bf16[4,80,2048]{2,1,0:T(8,128)(2,1)} %fusion.10), calls=%async_computation.3 | async-start | bytes 2621440 | tf_op jit(solution)/shard_map/all_to_all | solution.py:61
  1070.8 49.1 %collective-permute-start.56 = (bf16[2,4,64,1280]{3,2,1,0:T(8,128)(2,1)S(1)}, bf16[2,4,64,1280]{3,2,1,0:T(8,128)(2,1)S(1)}, u32[]{:S(2)}, u32[]{:S(2)}) collective-permute-start(bf16[2,4,64,1280]{3,2,1,0:T(8,128)(2,1)S(1)} %fusion.35), channel_id=1, source_target_pairs={{0,1},{1,0},{2,3},{3,2},{4,5},{5,4},{6,7},{7,6},{8,9},{9,8},{10,11... | collective-permute-start | bytes 3932168 | tf_op jit(solution)/shard_map/ppermute | solution.py:21
  1121.4 35.0 %all-to-all-start.2 = ((bf16[4,2,64,1280]{3,2,1,0:T(8,128)(2,1)}), bf16[4,2,64,1280]{3,2,1,0:T(8,128)(2,1)S(1)}, u32[]{:S(2)}, u32[]{:S(2)}) async-start(bf16[4,2,64,1280]{3,2,1,0:T(8,128)(2,1)} %copy.143), calls=%async_computation.2 | async-start | bytes 2621440 | tf_op jit(solution)/shard_map/all_to_all | solution.py:61
  1127.7 25.5 %collective-permute-start.53 = (bf16[2,4,64,1280]{3,2,1,0:T(8,128)(2,1)S(1)}, bf16[2,4,64,1280]{3,2,1,0:T(8,128)(2,1)S(1)}, u32[]{:S(2)}, u32[]{:S(2)}) collective-permute-start(bf16[2,4,64,1280]{3,2,1,0:T(8,128)(2,1)S(1)} %fusion.34), channel_id=1, source_target_pairs={{0,1},{1,0},{2,3},{3,2},{4,5},{5,4},{6,7},{7,6},{8,9},{9,8},{10,11... | collective-permute-start | bytes 3932168 | tf_op jit(solution)/shard_map/ppermute | solution.py:21
  1156.5 34.9 %all-to-all-start.1 = ((bf16[4,2,64,1280]{3,2,1,0:T(8,128)(2,1)}), bf16[4,2,64,1280]{3,2,1,0:T(8,128)(2,1)}, u32[]{:S(2)}, u32[]{:S(2)}) async-start(bf16[4,2,64,1280]{3,2,1,0:T(8,128)(2,1)} %copy.142), calls=%async_computation.1 | async-start | bytes 2621440 | tf_op jit(solution)/shard_map/all_to_all | solution.py:61
  (142 other events, 1685.0 us)

commit v2 on v1

--- a/solution.py
+++ b/solution.py
@@ -9,7 +9,7 @@
 from jax.sharding import PartitionSpec as P
 
 HB = 256
-EVERY = ("x", "core", "z", "y")
+EVERY = ("x", "core", "zh", "zl", "y")
 F32 = jnp.float32
 BF16 = jnp.bfloat16
 
@@ -27,39 +27,63 @@
     return lax.ppermute(block, axis, route)
 
 
+def after(value, *earlier):
+    return lax.optimization_barrier((value,) + earlier)[0]
+
+
+def pick(array, index, dim):
+    return lax.dynamic_index_in_dim(array, index, dim, keepdims=False)
+
+
+def received(block, axis):
+    return [block] + [rotated(block, axis, d) for d in range(1, lax.axis_size(axis))]
+
+
+def spread_near(block, axis, dim):
+    return jnp.stack(received(block, axis), axis=dim)
+
+
+def near(array, axis, dim):
+    count = lax.axis_size(axis)
+    place = lax.axis_index(axis)
+    if count == 2:
+        return jnp.where(place == 0, array, jnp.flip(array, dim))
+    return jnp.stack(
+        [pick(array, lax.rem(place - d + count, count), dim) for d in range(count)], axis=dim
+    )
+
+
 def spread(block, axis, dim):
     count = lax.axis_size(axis)
     place = lax.axis_index(axis)
+    pieces = received(block, axis)
     if count == 2:
-        other = rotated(block, axis, 1)
         low = place == 0
         return jnp.stack(
-            [jnp.where(low, block, other), jnp.where(low, other, block)], axis=dim
+            [jnp.where(low, pieces[0], pieces[1]), jnp.where(low, pieces[1], pieces[0])], axis=dim
         )
     shape = block.shape[:dim] + (count,) + block.shape[dim:]
     whole = jnp.zeros(shape, block.dtype)
-    for distance in range(count):
-        piece = block if distance == 0 else rotated(block, axis, distance)
-        source = lax.rem(place - distance + count, count)
-        whole = lax.dynamic_update_slice_in_dim(
-            whole, jnp.expand_dims(piece, dim), source, dim
-        )
+    for d, piece in enumerate(pieces):
+        source = lax.rem(place - d + count, count)
+        whole = lax.dynamic_update_slice_in_dim(whole, jnp.expand_dims(piece, dim), source, dim)
     return whole
 
 
-def pick(array, index, dim):
-    return lax.dynamic_index_in_dim(array, index, dim, keepdims=False)
+def collect_near(part, axis):
+    count = lax.axis_size(axis)
+    got = [rotated(part(d).astype(BF16), axis, count - d) for d in range(1, count)]
+    return sum([g.astype(F32) for g in got], part(0).astype(F32))
+
+
+def collect_dim(partial, axis, dim):
+    return collect_near(lambda d: lax.index_in_dim(partial, d, dim, keepdims=False), axis)
 
 
 def collect(partial, axis, dim):
     count = lax.axis_size(axis)
     place = lax.axis_index(axis)
-    if count == 2:
-        got = rotated(pick(partial, 1 - place, dim).astype(BF16), axis, 1)
-        return pick(partial, place, dim).astype(F32) + got.astype(F32)
-    blocks = jnp.moveaxis(partial, dim, 0).astype(BF16)
-    got = lax.all_to_all(blocks, axis, 0, 0)
-    return jnp.sum(got.astype(F32), axis=0)
+    return collect_near(lambda d: pick(partial, lax.rem(place - d + count, count), dim), axis)
 
 
 def pair_rows(block):
@@ -204,59 +228,150 @@
     return lax.dot_general(left, right, (((0,), (0,)), ((), ())), preferred_element_type=F32)
 
 
-def gather_rows(block):
-    rows, width = block.shape[1:]
-    block = spread(block, "z", 1)
-    block = spread(block, "y", 2)
-    block = spread(block, "x", 0)
-    return block.reshape(-1, width)
-
-
-def gather_half(block):
-    width = block.shape[1]
-    block = spread(block, "z", 0)
-    block = spread(block, "y", 1)
-    block = spread(block, "x", 0)
-    return block.reshape(-1, width)
-
-
-def gather_feed(block):
-    width = block.shape[1]
-    block = spread(block, "z", 0)
-    block = spread(block, "y", 1)
-    return block.reshape(-1, width)
+def sizes(*axes):
+    return tuple(lax.axis_size(axis) for axis in axes)
+
+
+def flat(block):
+    return block.reshape(-1, block.shape[-1])
+
+
+def mixer_order(values):
+    rows = values.shape[0]
+    values = values.reshape((rows,) + sizes(*EVERY) + (-1,))
+    for axis, dim in (("x", 1), ("zh", 3), ("zl", 4), ("y", 5)):
+        values = near(values, axis, dim)
+    return values.transpose(0, 2, 1, 5, 4, 3, 6).reshape(rows, -1)
+
+
+def mixer_order_back(values):
+    rows = values.shape[0]
+    values = values.reshape((rows,) + sizes("core", "x", "y", "zl", "zh") + (-1,))
+    values = values.transpose(0, 2, 1, 5, 4, 3, 6)
+    for axis, dim in (("x", 1), ("zh", 3), ("zl", 4), ("y", 5)):
+        values = near(values, axis, dim)
+    return values.reshape(rows, -1)
+
+
+def gather_rows(block, mark):
+    width = block.shape[2]
+    block = block if mark is None else after(block, mark)
+    pieces = received(block, "zh")
+    block = spread_near(jnp.stack(pieces, axis=1), "zl", 1)
+    one = spread_near(spread_near(block[0], "y", 0), "x", 0)
+    two = spread_near(spread_near(block[1], "x", 0), "y", 1)
+    return jnp.concatenate([one.reshape(-1, width), two.reshape(-1, width)], axis=0), pieces[1]
 
 
 def sum_rows(left, right, rows):
-    x_count, z_count, y_count = (lax.axis_size(a) for a in ("x", "z", "y"))
-    width = right.shape[1]
-    partial = outer(left, right).reshape(x_count, 2, z_count, y_count, rows, width)
-    partial = collect(partial, "x", 0)
+    x_count, y_count, l_count, h_count = sizes("x", "y", "zl", "zh")
+    batch_rows = l_count * h_count * rows
+    parts = left.shape[0], 2, x_count, y_count, batch_rows
+
+    def part(c, x, y):
+        start = ((c * x_count + x) * y_count + y) * batch_rows
+        return left[:, start : start + batch_rows]
+
+    def first_x(x):
+        start = x * y_count * batch_rows
+        return outer(left[:, start : start + y_count * batch_rows], right)
+
+    def first_y(y):
+        return jnp.concatenate([outer(part(1, x, y), right) for x in range(x_count)], axis=0)
+
+    one = collect_near(first_x, "x").reshape(y_count, l_count, h_count, rows, -1)
+    two = collect_near(first_y, "y").reshape(x_count, l_count, h_count, rows, -1)
+    both = jnp.stack([collect_dim(one, "y", 0), collect_dim(two, "x", 0)], axis=2)
+    return collect_dim(collect_dim(both, "zl", 0), "zh", 0)
+
+
+def along_batch(block, mark):
+    pieces = after(block, mark)
+    block = spread(pieces, "zh", 0)
+    arrived = block
+    return spread(spread(block, "zl", 1), "y", 2), arrived
+
+
+def pieces_of_x(block):
+    count = lax.axis_size("x")
+    place = lax.axis_index("x")
+    return [
+        (flat(piece), lax.rem(place - d + count, count))
+        for d, piece in enumerate(received(block, "x"))
+    ]
+
+
+def columns_of(values, place, width):
+    return lax.dynamic_slice_in_dim(values, place * width, width, 1)
+
+
+def times_pieces(values, pieces):
+    width = pieces[0][0].shape[0]
+    return sum(dot(columns_of(values, place, width), piece) for piece, place in pieces)
+
+
+def times_pieces_t(values, pieces):
+    parts = jnp.stack([dot_t(values, piece) for piece, place in pieces], axis=1)
+    return near(parts, "x", 1).reshape(values.shape[0], -1)
+
+
+def sum_half(part, rows):
+    h_count, l_count, y_count = sizes("zh", "zl", "y")
+    count = lax.axis_size("x")
+    place = lax.axis_index("x")
+    partial = collect_near(lambda d: part(lax.rem(place - d + count, count)), "x")
+    partial = partial.reshape(h_count, l_count, y_count, rows, partial.shape[-1])
     partial = collect(partial, "y", 2)
-    return collect(partial, "z", 1)
-
-
-def sum_half(partial, rows):
-    x_count, z_count, y_count = (lax.axis_size(a) for a in ("x", "z", "y"))
+    partial = collect(partial, "zl", 1)
+    return from_half(collect(partial, "zh", 0).astype(BF16)).astype(F32)
+
+
+def split_feed(block):
+    rows, width = block.shape[0], block.shape[1] // 2
+    halves = block.reshape(rows, 2, width)
+    place = lax.axis_index("y")
+    own = pick(halves, place, 1)
+    other = rotated(pick(halves, 1 - place, 1), "y", 1)
+    low = place == 0
+    return jnp.stack([jnp.where(low, own, other), jnp.where(low, other, own)], axis=0)
+
+
+def unsplit_feed(block):
+    place = lax.axis_index("y")
+    own = pick(block, place, 0)
+    other = rotated(pick(block, 1 - place, 0).astype(BF16), "y", 1).astype(F32)
+    low = place == 0
+    return jnp.concatenate([jnp.where(low, own, other), jnp.where(low, other, own)], axis=1)
+
+
+def gather_feed(block, mark):
+    block = after(flat(block), mark)
+    return lax.all_gather(block, ("zh", "zl"), axis=0, tiled=True)
+
+
+def sum_feed(left, right):
+    total = outer(left, right).astype(BF16)
+    total = lax.psum_scatter(total, ("zh", "zl"), scatter_dimension=0, tiled=True)
+    return unsplit_feed(total.reshape(2, -1, right.shape[1]).astype(F32))
+
+
+def everyones_rows(block):
+    middle = block.shape[0] // 2
+    one = spread_near(spread_near(block[:middle], "x", 0), "y", 0)
+    two = spread_near(spread_near(block[middle:], "y", 0), "x", 0)
+    return flat(spread_near(jnp.concatenate([flat(one), flat(two)], axis=0), "core", 0))
+
+
+def owners_rows(partial):
+    x_count, y_count = sizes("x", "y")
     width = partial.shape[1]
-    partial = partial.reshape(x_count, z_count, y_count, rows, width)
-    partial = collect(partial, "x", 0)
-    partial = collect(partial, "y", 1)
-    return from_half(collect(partial, "z", 0).astype(BF16)).astype(F32)
-
-
-def sum_feed(left, right):
-    z_count, y_count = lax.axis_size("z"), lax.axis_size("y")
-    rows, width = left.shape[1] // (z_count * y_count), right.shape[1]
-    place = lax.axis_index("y")
-    columns = left.reshape(left.shape[0], z_count, y_count, rows)
-
-    def part(which):
-        return outer(pick(columns, which, 2).reshape(left.shape[0], z_count * rows), right)
-
-    got = rotated(part(1 - place).astype(BF16), "y", 1)
-    total = part(place) + got.astype(F32)
-    return collect(total.reshape(z_count, rows, width), "z", 0)
+    block = collect_dim(partial.reshape(2, -1, width), "core", 0)
+    middle = block.shape[0] // 2
+    one = block[:middle].reshape(y_count, x_count, -1, width)
+    two = block[middle:].reshape(x_count, y_count, -1, width)
+    one = collect_dim(collect_dim(one, "y", 0), "x", 0)
+    two = collect_dim(collect_dim(two, "x", 0), "y", 0)
+    return jnp.concatenate([one, two], axis=0)
 
 
 def on_device(
@@ -279,7 +394,7 @@
     feed_up,
     feed_down,
 ):
-    x_count, z_count, y_count = (lax.axis_size(a) for a in ("x", "z", "y"))
+    x_count = lax.axis_size("x")
     x_place, core = lax.axis_index("x"), lax.axis_index("core")
     own_rows, model = tokens.shape[1:]
     channels = conv_kernel.shape[1]
@@ -314,31 +429,33 @@
         by_channel[7],
     )
 
-    input_full = gather_rows(swap_columns(input_proj))
-    branch_full = gather_rows(swap_columns(branch_proj))
-    gates_full = gather_half(to_half(jnp.concatenate([recur_gate, inlet_gate], axis=1)))
-    recur_full, inlet_full = gates_full[:, :HB], gates_full[:, HB:]
-    output_full = gather_half(to_half(output_proj))
-    gate_local = gather_feed(feed_gate)
-    lin_local = gather_feed(feed_up)
-    down_local = gather_feed(feed_down.T)
-
-    grad_out = cotangent[0].astype(F32)
-    grad_feed = (validity * grad_out).astype(BF16)
-    everyones_rows = lambda block: spread(spread(block, "x", 0), "core", 1).reshape(-1, model)
-    grad_all = everyones_rows(grad_feed)
-
     channel_rate = jax.nn.softplus(param_wide)
     token_rows = tokens[0].astype(F32)
     factor_one = rms_factor(token_rows)
     scaled_one = token_rows * factor_one
-    normed = pair_rows((scaled_one * gain_one).astype(BF16))
+    normed = pair_rows(mixer_order((scaled_one * gain_one).astype(BF16)))
     rows = normed.shape[0]
+    rim_normed = shifted(normed[rows - 8 :], "x", 1).reshape(8, 2, x_count, -1)
+    rim_normed = jnp.roll(rim_normed, 1, axis=2).reshape(8, model)
+    extended_normed = jnp.concatenate([rim_normed, normed], axis=0)
+
+    input_full, mark = gather_rows(swap_columns(input_proj), None)
+    gates = to_half(jnp.concatenate([recur_gate, inlet_gate], axis=1))
+    gates_full = lax.all_gather(gates, ("x", "zh", "zl", "y"), axis=0, tiled=True)
+    recur_full, inlet_full = gates_full[:, :HB], gates_full[:, HB:]
+    branch_full, mark = gather_rows(swap_columns(branch_proj), mark)
+    output_rows, mark = along_batch(to_half(output_proj), mark)
+    output_full = pieces_of_x(output_rows)
+    gate_local = gather_feed(split_feed(feed_gate), mark)
+    lin_local = gather_feed(split_feed(feed_up), mark)
+    down_local = gather_feed(split_feed(feed_down.T), mark)
+
+    grad_out = cotangent[0].astype(F32)
+    grad_feed = (validity * grad_out).astype(BF16)
+    grad_all = everyones_rows(grad_feed)
+
     branch = dot(normed, branch_full)
-    inner_proj = dot(normed, input_full).astype(BF16)
-    rim_rows = shifted(inner_proj[rows - 3 :], "x", 1)
-    extended = jnp.concatenate([rim_rows, inner_proj], axis=0)
-    extended_wide = extended.astype(F32)
+    extended_wide = dot(extended_normed, input_full)[5:].astype(BF16).astype(F32)
     convolved = bias_conv + kernel_wide[0] * extended_wide[3 : 3 + rows]
     for offset in range(1, 4):
         convolved = convolved + kernel_wide[offset] * extended_wide[3 - offset : 3 - offset + rows]
@@ -356,7 +473,7 @@
     states = local_state + cumulative * state_in
     gate_values = gelu_tanh(branch)
     mixed_in = (gate_values * states).astype(BF16)
-    mix = pair_sum(dot(mixed_in, output_full))
+    mix = pair_sum(times_pieces(mixed_in, output_full))
     middle = token_rows + validity * mix
     factor_two = rms_factor(middle)
     scaled_two = middle * factor_two
@@ -372,23 +489,23 @@
     grad_pre = gelu_pull(grad_hidden * feed_lin)[0].astype(BF16)
     grad_lin = (grad_hidden * feed_act).astype(BF16)
     grad_rows = dot_t(grad_pre, gate_local) + dot_t(grad_lin, lin_local)
-
-    def owners_rows(partial):
-        block = partial.reshape(x_count, 2, own_rows, model)
-        block = pick(block, core, 1) + rotated(pick(block, 1 - core, 1), "core", 1)
-        return collect(block, "x", 0)
-
     grad_normed_two = owners_rows(grad_rows)
-    feed_out = owners_rows(dot_t(hidden, down_local))
-    output = (middle + validity * feed_out).astype(BF16)[None]
-    feed_grad_gate = sum_feed(all_rows, grad_pre)
-    feed_grad_up = sum_feed(all_rows, grad_lin)
+    later_rows, grad_pre, grad_lin = lax.optimization_barrier(
+        (all_rows, grad_pre, grad_lin, grad_rows)
+    )[:3]
+    feed_grad_gate = sum_feed(later_rows, grad_pre)
+    feed_grad_up = sum_feed(later_rows, grad_lin)
 
     grad_mid_norm, grad_gain_feed = norm_backward(grad_normed_two, scaled_two, factor_two, gain_two)
     grad_middle = grad_out + grad_mid_norm
     grad_mix = pair_rows((validity * grad_middle).astype(BF16))
-    grad_output = sum_half(outer(mixed_in, grad_mix), output_proj.shape[0])
-    grad_mixed = dot_t(grad_mix, output_full)
+    per_x = mixed_in.shape[1] // x_count
+    grad_output = sum_half(
+        lambda place: outer(columns_of(mixed_in, place, per_x), grad_mix), output_proj.shape[0]
+    )
+    feed_out = owners_rows(dot_t(after(hidden, grad_mix), down_local))
+    output = (middle + validity * feed_out).astype(BF16)[None]
+    grad_mixed = times_pieces_t(grad_mix, output_full)
     grad_branch = jax.vjp(gelu_tanh, branch)[1](grad_mixed * states)[0].astype(BF16)
     grad_branch_proj = unswap_columns(sum_rows(normed, grad_branch, branch_proj.shape[0]))
     grad_states = grad_mixed * gate_values
@@ -406,11 +523,11 @@
     grad_param = jnp.sum(grad_log * (-8.0 * recurrence), axis=0) * jax.nn.sigmoid(param_wide)
     rounded_recur = grad_recur_pre.astype(BF16)
     rounded_inlet = grad_inlet_pre.astype(BF16)
+    grad_gates_here = jnp.concatenate(
+        [head_outer(conv_low, rounded_recur), head_outer(conv_low, rounded_inlet)], axis=1
+    )
     grad_gates = sum_half(
-        jnp.concatenate(
-            [head_outer(conv_low, rounded_recur), head_outer(conv_low, rounded_inlet)], axis=1
-        ),
-        channels,
+        lambda place: lax.dynamic_slice_in_dim(grad_gates_here, place * per_x, per_x, 0), channels
     )
     grad_conv = (
         carried * scaling * inlets
@@ -431,7 +548,9 @@
         ],
         axis=0,
     )
-    grad_normed = pair_sum(dot_t(grad_inner, input_full) + dot_t(grad_branch, branch_full))
+    grad_normed = mixer_order_back(
+        pair_sum(dot_t(grad_inner, input_full) + dot_t(grad_branch, branch_full))
+    )
     grad_token_norm, grad_gain_mixer = norm_backward(grad_normed, scaled_one, factor_one, gain_one)
     grad_tokens = (grad_middle + grad_token_norm)[None]
 
@@ -483,8 +602,8 @@
 
 def solution(mesh):
     seq, batch = mesh.shape["seq"], mesh.shape["batch"]
-    fine = Mesh(mesh.devices.reshape(seq // 2, 2, batch // 2, 2), EVERY)
-    sequences, places = ("z", "y"), ("x", "core")
+    fine = Mesh(mesh.devices.reshape(seq // 2, 2, batch // 4, 2, 2), EVERY)
+    sequences, places = ("zh", "zl", "y"), ("x", "core")
     rows = P(sequences, places, None)
     spread_rows, spread_columns, spread_all = P(EVERY, None), P(None, EVERY), P(EVERY)
     feed = P(sequences, places)

time: 1210 us -> 822 us (0.68)
  waiting for transfers between devices: 685 us -> 330 us
  local copies, waits for them, and re-layouts: 145 us -> 88.6 us
  between operations: 3.72 us -> 17.7 us
    ppermute x59 -> x70, waiting for transfers between devices: 633 us -> 246 us  [rotated(): lax.ppermute(block, axis, [(i, (i + distance) % count) for i in range(cou...]
    ppermute x4, waiting for transfers between devices: 0.72 us -> 61 us  [shifted(): return lax.ppermute(block, axis, route)]
    all_to_all x1, waiting for transfers between devices: 37.5 us -> 0.01 us  [share_small(): lax.all_to_all(jnp.broadcast_to(vector[None], (count,) + vector.shape), E...]
    ppermute x59 -> x70, starting transfers between devices: 59.6 us -> 92.8 us  [rotated(): lax.ppermute(block, axis, [(i, (i + distance) % count) for i in range(cou...]
    all_to_all x7 -> x0, starting transfers between devices: 30.8 us -> none  [collect(): got = lax.all_to_all(blocks, axis, 0, 0)]
    dynamic_slice x7, local copies, waits for them, and re-layouts: 36 us -> 11.2 us  [pick(): return lax.dynamic_index_in_dim(array, index, dim, keepdims=False)]
    ppermute x2, waiting for transfers between devices: 2.33 us -> 23 us  [from_half(): return lax.ppermute(block, ('x', 'core'), [(b, a) for a, b in half_route()])]
    another operation x10 -> x5, local copies, waits for them, and re-layouts: 17.4 us -> 0.91 us  [spread_near(): return jnp.stack(received(block, axis), axis=dim)]
  transfers between devices with their start and end apart: 76 -> 87, of which waited for: 40 -> 34; matrix products, arithmetic and copies ran while one was open for 26% -> 33% of each run, Pallas kernels for 0% -> 1%
where the time goes in v2:
time: 822 us; the launch traced here: 811 us
  waiting for transfers between devices  330 us (40%)
  starting transfers between devices  148 us (18%)
  other arithmetic  120 us (15%)
  matrix products  102 us (12%)
  local copies, waits for them, and re-layouts  88.6 us (11%)
  between operations  17.7 us (2%)
    ppermute x70, waiting for transfers between devices, rotated(): lax.ppermute(block, axis, [(i, (i + distance) % count) for i in range(cou...  246 us
    ppermute x70, starting transfers between devices, rotated(): lax.ppermute(block, axis, [(i, (i + distance) % count) for i in range(cou...  92.8 us
    ppermute x4, waiting for transfers between devices, shifted(): return lax.ppermute(block, axis, route)  61 us
    dot_general x7, matrix products, dot(): return jnp.dot(left, right, preferred_element_type=F32)  35.3 us
    dot_general x17, matrix products, outer(): lax.dot_general(left, right, (((0,), (0,)), ((), ())), preferred_element_...  35 us
    unnamed x234, local copies, waits for them, and re-layouts  30.5 us
    another operation x24, other arithmetic, spread_near(): return jnp.stack(received(block, axis), axis=dim)  25.8 us
    ppermute x2, waiting for transfers between devices, from_half(): return lax.ppermute(block, ('x', 'core'), [(b, a) for a, b in half_route()])  23 us
  transfers between devices with their start and end apart: 87, of which 34 were waited for; matrix products, arithmetic and copies ran while one was open for 33% of the time, Pallas kernels for 1%

profile of v2, /device:TPU:1, one launch (start us, length us, event | category | flops | bytes accessed | tf_op | source)
XLA Modules:
  0.0 811.0 jit_solution(14768223191156021340)
XLA Ops:
  12.7 4.5 collective-permute-start.10
  27.9 14.9 %collective-permute-done.3 = bf16[2,64,1280]{2,1,0:T(8,128)(2,1)S(1)} collective-permute-done((bf16[2,64,1280]{2,1,0:T(8,128)(2,1)S(1)}, bf16[2,64,1280]{2,1,0:T(8,128)(2,1)S(1)}, u32[]{:S(2)}, u32[]{:S(2)}) %collective-permute-start.3) | collective-permute-done | bytes 327712 | tf_op jit(solution)/shard_map/ppermute | solution.py:21
  46.0 8.5 %all-to-all-start = ((bf16[32,2,384]{2,1,0:T(2,128)(2,1)}), bf16[32,2,384]{2,1,0:T(2,128)(2,1)S(1)}, u32[]{:S(2)}, u32[]{:S(2)}) async-start(bf16[32,2,384]{2,1,0:T(2,128)(2,1)} %reshape.518), calls=%async_computation | async-start | bytes 98304 | tf_op jit(solution)/shard_map/all_to_all | solution.py:133
  54.9 5.1 collective-permute-done.4
  63.2 15.4 %collective-permute-done.19 = bf16[80,2048]{1,0:T(8,128)(2,1)S(1)} collective-permute-done((bf16[80,2048]{1,0:T(8,128)(2,1)}, bf16[80,2048]{1,0:T(8,128)(2,1)S(1)}, u32[]{:S(2)}, u32[]{:S(2)}) %collective-permute-start.19) | collective-permute-done | bytes 327712 | tf_op jit(solution)/shard_map/ppermute | solution.py:21
  89.6 6.4 collective-permute-done.29
  100.3 3.2 collective-permute-start.11
  105.4 22.1 %collective-permute-done.12 = bf16[2,2,64,1280]{3,2,0,1:T(8,128)(2,1)S(1)} collective-permute-done((bf16[2,2,64,1280]{3,2,0,1:T(8,128)(2,1)S(1)}, bf16[2,2,64,1280]{3,2,0,1:T(8,128)(2,1)S(1)}, u32[]{:S(2)}, u32[]{:S(2)}) %collective-permute-start.12) | collective-permute-done | bytes 655392 | tf_op jit(solution)/shard_map/ppermute | solution.py:21
  131.5 33.4 %collective-permute-done.5 = bf16[2,2,64,1280]{3,2,1,0:T(8,128)(2,1)} collective-permute-done((bf16[2,2,64,1280]{3,2,1,0:T(8,128)(2,1)}, bf16[2,2,64,1280]{3,2,1,0:T(8,128)(2,1)}, u32[]{:S(2)}, u32[]{:S(2)}) %collective-permute-start.5) | collective-permute-done | bytes 655392 | tf_op jit(solution)/shard_map/ppermute | solution.py:21
  176.7 14.7 %collective-permute-done.20 = bf16[2,80,2048]{2,1,0:T(8,128)(2,1)} collective-permute-done((bf16[2,80,2048]{2,1,0:T(8,128)(2,1)}, bf16[2,80,2048]{2,1,0:T(8,128)(2,1)}, u32[]{:S(2)}, u32[]{:S(2)}) %collective-permute-start.20) | collective-permute-done | bytes 655392 | tf_op jit(solution)/shard_map/ppermute | solution.py:21
  215.6 18.9 %collective-permute-done.21 = bf16[2,2,80,2048]{3,2,1,0:T(8,128)(2,1)} collective-permute-done((bf16[2,2,80,2048]{3,2,1,0:T(8,128)(2,1)}, bf16[2,2,80,2048]{3,2,1,0:T(8,128)(2,1)}, u32[]{:S(2)}, u32[]{:S(2)}) %collective-permute-start.21) | collective-permute-done | bytes 1310752 | tf_op jit(solution)/shard_map/ppermute | solution.py:21
  255.8 6.8 collective-permute-done.9
  264.4 26.0 %collective-permute-done.17 = f32[1280]{0:T(1024)S(1)} collective-permute-done((f32[1280]{0:T(1024)S(1)}, f32[1280]{0:T(1024)S(1)}, u32[]{:S(2)}, u32[]{:S(2)}) %collective-permute-start.17) | collective-permute-done | bytes 5152 | tf_op jit(solution)/shard_map/ppermute | solution.py:27
  290.4 3.3 multiply_convert_fusion.2
  297.2 14.7 %collective-permute-start.23 = (f32[128,2048]{1,0:T(8,128)}, f32[128,2048]{1,0:T(8,128)}, u32[]{:S(2)}, u32[]{:S(2)}) collective-permute-start(f32[128,2048]{1,0:T(8,128)} %dynamic-slice_bitcast_fusion), channel_id=1, source_target_pairs={{0,8},{8,0},{1,9},{9,1},{2,10},{10,2},{3,11},{11,3},{4,12},{12,4},... | collective-permute-start | bytes 3145736 | tf_op jit(solution)/shard_map/ppermute | solution.py:21
  314.7 8.8 %reduce-scatter.8.cloned.1.call-start = ((), (), s32[]{:S(2)}) async-start(), calls=%async_computation.11 | async-start | bytes 3932160 | tf_op jit(solution)/shard_map/reduce_scatter | solution.py:354
  330.5 4.3 collective-permute-done.31
  343.6 9.4 %collective-permute-done.32 = bf16[2,64,2048]{2,1,0:T(8,128)(2,1)S(1)} collective-permute-done((bf16[2,64,2048]{2,1,0:T(8,128)(2,1)S(1)}, bf16[2,64,2048]{2,1,0:T(8,128)(2,1)S(1)}, u32[]{:S(2)}, u32[]{:S(2)}) %collective-permute-start.32) | collective-permute-done | bytes 524320 | tf_op jit(solution)/shard_map/ppermute | solution.py:21
  354.7 9.5 %collective-permute-done.25 = bf16[2,64,2048]{2,1,0:T(8,128)(2,1)S(1)} collective-permute-done((bf16[2,64,2048]{2,1,0:T(8,128)(2,1)S(1)}, bf16[2,64,2048]{2,1,0:T(8,128)(2,1)S(1)}, u32[]{:S(2)}, u32[]{:S(2)}) %collective-permute-start.25) | collective-permute-done | bytes 524320 | tf_op jit(solution)/shard_map/ppermute | solution.py:21
  371.8 8.2 %fusion.166 = f32[1024,768]{1,0:T(8,128)} fusion(bf16[1024,2048]{1,0:T(8,128)(2,1)} %bitcast.525, bf16[2048,768]{1,0:T(8,128)(2,1)} %all-gather.9.cloned.1.call-done), kind=kOutput, calls=%fused_computation.421 | convolution fusion | flops 3221225472 | bytes 10485760 | tf_op jit(solution)/shard_map/dot_general | solution.py:220
  380.1 8.3 %fusion.165 = f32[1024,768]{1,0:T(8,128)} fusion(bf16[1024,2048]{1,0:T(8,128)(2,1)} %bitcast.526, bf16[2048,768]{1,0:T(8,128)(2,1)} %all-gather.7.cloned.1.call-done), kind=kOutput, calls=%fused_computation.420 | convolution fusion | flops 3221225472 | bytes 10485760 | tf_op jit(solution)/shard_map/dot_general | solution.py:220
  388.4 11.8 %multiply_convert_fusion = (bf16[1024,768]{1,0:T(8,128)(2,1)S(1)}, bf16[1024,768]{1,0:T(8,128)(2,1)}, bf16[1024,768]{1,0:T(8,128)(2,1)S(1)}) fusion(f32[1024,768]{1,0:T(8,128)} %fusion.165, f32[1024,768]{1,0:T(8,128)} %fusion.166, bf16[1024,2048]{1,0:T(8,128)(2,1)} %bitcast.529, bf16[2048,768]{1,0:T(8,128)(2,1)} %all-gather.11.cloned.1.call-done), kind=kOutput, calls=%fused_computation.27 | convolution fusion | flops 3241672704 | bytes 18350080 | tf_op jit(solution)/shard_map/dot_general | solution.py:220
  401.3 5.1 convolution_convert_fusion
  406.4 6.0 fusion.167
  412.4 3.5 convolution_add_fusion
  416.0 3.3 copy-done.49
  423.6 6.3 convolution_convert_fusion.1
  430.4 3.7 fusion.151
  436.0 11.6 %collective-permute-done.38 = bf16[2,64,2048]{2,1,0:T(8,128)(2,1)S(1)} collective-permute-done((bf16[2,64,2048]{2,1,0:T(8,128)(2,1)S(1)}, bf16[2,64,2048]{2,1,0:T(8,128)(2,1)S(1)}, u32[]{:S(2)}, u32[]{:S(2)}) %collective-permute-start.38) | collective-permute-done | bytes 524320 | tf_op jit(solution)/shard_map/ppermute | solution.py:21
  450.0 5.0 collective-permute-done.39
  460.4 4.9 convolution_convert_fusion.2
  489.4 3.4 fusion.168
  523.3 5.6 multiply_reduce_fusion.1
  536.6 35.0 %collective-permute-done.49 = f32[3,1280]{1,0:T(4,128)S(1)} collective-permute-done((f32[3,1280]{1,0:T(4,128)S(1)}, f32[3,1280]{1,0:T(4,128)S(1)}, u32[]{:S(2)}, u32[]{:S(2)}) %collective-permute-start.49) | collective-permute-done | bytes 15392 | tf_op jit(solution)/shard_map/ppermute | solution.py:27
  572.3 4.2 fusion
  583.8 3.9 collective-permute-start.50
  599.0 3.4 collective-permute-done.71
  609.7 6.7 all-to-all-start.1
  632.3 5.4 collective-permute-start.74
  641.0 19.1 %collective-permute-done.74 = bf16[80,512]{1,0:T(8,128)(2,1)S(1)} collective-permute-done((bf16[80,512]{1,0:T(8,128)(2,1)S(1)}, bf16[80,512]{1,0:T(8,128)(2,1)S(1)}, u32[]{:S(2)}, u32[]{:S(2)}) %collective-permute-start.74) | collective-permute-done | bytes 81952 | tf_op jit(solution)/shard_map/ppermute | solution.py:128
  666.9 10.1 %collective-permute-done.61 = bf16[2,2,64,1280]{3,2,1,0:T(8,128)(2,1)S(1)} collective-permute-done((bf16[2,2,64,1280]{3,2,1,0:T(8,128)(2,1)S(1)}, bf16[2,2,64,1280]{3,2,1,0:T(8,128)(2,1)S(1)}, u32[]{:S(2)}, u32[]{:S(2)}) %collective-permute-start.61) | collective-permute-done | bytes 655392 | tf_op jit(solution)/shard_map/ppermute | solution.py:21
  680.9 8.8 %collective-permute-done.54 = bf16[2,2,64,1280]{3,2,1,0:T(8,128)(2,1)S(1)} collective-permute-done((bf16[2,2,64,1280]{3,2,1,0:T(8,128)(2,1)S(1)}, bf16[2,2,64,1280]{3,2,1,0:T(8,128)(2,1)S(1)}, u32[]{:S(2)}, u32[]{:S(2)}) %collective-permute-start.54) | collective-permute-done | bytes 655392 | tf_op jit(solution)/shard_map/ppermute | solution.py:21
  704.5 4.4 collective-permute-done.44
  722.7 20.1 %collective-permute-done.47 = bf16[64,2048]{1,0:T(8,128)(2,1)} collective-permute-done((bf16[64,2048]{1,0:T(8,128)(2,1)}, bf16[64,2048]{1,0:T(8,128)(2,1)}, u32[]{:S(2)}, u32[]{:S(2)}) %collective-permute-start.47) | collective-permute-done | bytes 262176 | tf_op jit(solution)/shard_map/ppermute | solution.py:21
  747.3 6.1 collective-permute-start.64
  780.9 6.9 collective-permute-done.68
  787.9 10.2 %collective-permute-start.69 = (bf16[80,2048]{1,0:T(8,128)(2,1)S(1)}, bf16[80,2048]{1,0:T(8,128)(2,1)S(1)}, u32[]{:S(2)}, u32[]{:S(2)}) collective-permute-start(bf16[80,2048]{1,0:T(8,128)(2,1)S(1)} %fusion.67), channel_id=1, source_target_pairs={{0,0},{16,8},{8,16},{24,24},{1,1},{17,9},{9,17},{25,25},{2,2},{18,... | collective-permute-start | bytes 983048 | tf_op jit(solution)/shard_map/ppermute | solution.py:128
  799.0 3.9 collective-permute-done.69
  (654 shorter events, 328.4 us)
Async XLA Ops:
  7.2 193.3 %all-gather.5.cloned.1.call-start = ((), (), s32[]{:S(2)}) async-start(), calls=%async_computation.5 | async-start | bytes 1392640 | tf_op jit(solution)/shard_map/all_gather | solution.py:444
  17.2 37.7 %collective-permute-start.18 = (bf16[80,2048]{1,0:T(8,128)(2,1)}, bf16[80,2048]{1,0:T(8,128)(2,1)}, u32[]{:S(2)}, u32[]{:S(2)}) collective-permute-start(bf16[80,2048]{1,0:T(8,128)(2,1)} %param.23), channel_id=1, source_target_pairs={{0,0},{8,16},{16,8},{24,24},{1,1},{9,17},{17,9},{25,25},{2,2},{10,... | collective-permute-start | bytes 983048 | tf_op jit(solution)/shard_map/ppermute | solution.py:124
  21.8 38.3 %collective-permute-start.30 = (bf16[256,768]{1,0:T(8,128)(2,1)}, bf16[256,768]{1,0:T(8,128)(2,1)}, u32[]{:S(2)}, u32[]{:S(2)}) collective-permute-start(bf16[256,768]{1,0:T(8,128)(2,1)} %bitcast.458), channel_id=1, source_target_pairs={{0,1},{1,0},{2,3},{3,2},{4,5},{5,4},{6,7},{7,6},{8,9},{9,8},{10,11... | collective-permute-start | bytes 1179656 | tf_op jit(solution)/shard_map/ppermute | solution.py:21
  24.1 35.9 %collective-permute-start.36 = (bf16[256,768]{1,0:T(8,128)(2,1)}, bf16[256,768]{1,0:T(8,128)(2,1)}, u32[]{:S(2)}, u32[]{:S(2)}) collective-permute-start(bf16[256,768]{1,0:T(8,128)(2,1)} %bitcast.113), channel_id=1, source_target_pairs={{0,1},{1,0},{2,3},{3,2},{4,5},{5,4},{6,7},{7,6},{8,9},{9,8},{10,11... | collective-permute-start | bytes 1179656 | tf_op jit(solution)/shard_map/ppermute | solution.py:21
  46.0 38.6 %all-to-all-start = ((bf16[32,2,384]{2,1,0:T(2,128)(2,1)}), bf16[32,2,384]{2,1,0:T(2,128)(2,1)S(1)}, u32[]{:S(2)}, u32[]{:S(2)}) async-start(bf16[32,2,384]{2,1,0:T(2,128)(2,1)} %reshape.518), calls=%async_computation | async-start | bytes 98304 | tf_op jit(solution)/shard_map/all_to_all | solution.py:133
  54.5 317.3 %all-gather.9.cloned.1.call-start = ((), (), s32[]{:S(2)}) async-start(), calls=%async_computation.7 | async-start | bytes 3932160 | tf_op jit(solution)/shard_map/all_gather | solution.py:349
  80.5 299.6 %all-gather.7.cloned.1.call-start = ((), (), s32[]{:S(2)}) async-start(), calls=%async_computation.6 | async-start | bytes 3932160 | tf_op jit(solution)/shard_map/all_gather | solution.py:349
  97.3 30.2 %collective-permute-start.12 = (bf16[2,2,64,1280]{3,2,0,1:T(8,128)(2,1)S(1)}, bf16[2,2,64,1280]{3,2,0,1:T(8,128)(2,1)S(1)}, u32[]{:S(2)}, u32[]{:S(2)}) collective-permute-start(bf16[2,2,64,1280]{3,2,0,1:T(8,128)(2,1)S(1)} %get-tuple-element.229), channel_id=1, source_target_pairs={{0,2},{2,0},{1,3},{3,1},{4,6},{6,4},{5,7},{7,5},{8,10},{10,8},{9,1... | collective-permute-start | bytes 1966088 | tf_op jit(solution)/shard_map/ppermute | solution.py:21
  100.3 29.6 %collective-permute-start.11 = (bf16[8,2048]{1,0:T(8,128)(2,1)S(1)}, bf16[8,2048]{1,0:T(8,128)(2,1)S(1)}, u32[]{:S(2)}, u32[]{:S(2)}) collective-permute-start(bf16[8,2048]{1,0:T(8,128)(2,1)S(1)} %slice.473), channel_id=1, source_target_pairs={{0,16},{1,17},{2,18},{3,19},{4,20},{5,21},{6,22},{7,23},{8,24},{9,... | collective-permute-start | bytes 98312 | tf_op jit(solution)/shard_map/ppermute | solution.py:27
  105.4 59.6 %collective-permute-start.5 = (bf16[2,2,64,1280]{3,2,1,0:T(8,128)(2,1)}, bf16[2,2,64,1280]{3,2,1,0:T(8,128)(2,1)}, u32[]{:S(2)}, u32[]{:S(2)}) collective-permute-start(bf16[2,2,64,1280]{3,2,1,0:T(8,128)(2,1)} %get-tuple-element.231), channel_id=1, source_target_pairs={{0,2},{2,0},{1,3},{3,1},{4,6},{6,4},{5,7},{7,5},{8,10},{10,8},{9,1... | collective-permute-start | bytes 1966088 | tf_op jit(solution)/shard_map/ppermute | solution.py:21
  128.6 40.4 %collective-permute-start.13 = (bf16[2,2,64,1280]{3,2,1,0:T(8,128)(2,1)}, bf16[2,2,64,1280]{3,2,1,0:T(8,128)(2,1)S(1)}, u32[]{:S(2)}, u32[]{:S(2)}) collective-permute-start(bf16[2,2,64,1280]{3,2,1,0:T(8,128)(2,1)} %bitcast.42), channel_id=1, source_target_pairs={{0,1},{1,0},{2,3},{3,2},{4,5},{5,4},{6,7},{7,6},{8,9},{9,8},{10,11... | collective-permute-start | bytes 1966088 | tf_op jit(solution)/shard_map/ppermute | solution.py:21
  129.9 42.5 %collective-permute-start.15 = (bf16[2,2,64,1280]{3,2,1,0:T(8,128)(2,1)}, bf16[2,2,64,1280]{3,2,1,0:T(8,128)(2,1)}, u32[]{:S(2)}, u32[]{:S(2)}) collective-permute-start(bf16[2,2,64,1280]{3,2,1,0:T(8,128)(2,1)} %bitcast.47), channel_id=1, source_target_pairs={{0,16},{16,0},{1,17},{17,1},{2,18},{18,2},{3,19},{19,3},{4,20},{20... | collective-permute-start | bytes 1966088 | tf_op jit(solution)/shard_map/ppermute | solution.py:21
  131.2 60.3 %collective-permute-start.20 = (bf16[2,80,2048]{2,1,0:T(8,128)(2,1)}, bf16[2,80,2048]{2,1,0:T(8,128)(2,1)}, u32[]{:S(2)}, u32[]{:S(2)}) collective-permute-start(bf16[2,80,2048]{2,1,0:T(8,128)(2,1)} %pad_maximum_fusion.44), channel_id=1, source_target_pairs={{0,2},{2,0},{1,3},{3,1},{4,6},{6,4},{5,7},{7,5},{8,10},{10,8},{9,1... | collective-permute-start | bytes 1966088 | tf_op jit(solution)/shard_map/ppermute | solution.py:21
  131.2 257.1 %all-gather.11.cloned.1.call-start = ((), (), s32[]{:S(2)}) async-start(), calls=%async_computation.8 | async-start | bytes 3932160 | tf_op jit(solution)/shard_map/all_gather | solution.py:349
  166.1 28.7 %collective-permute-start.6 = (bf16[2,2,64,1280]{3,2,1,0:T(8,128)(2,1)S(1)}, bf16[2,2,64,1280]{3,2,1,0:T(8,128)(2,1)S(1)}, u32[]{:S(2)}, u32[]{:S(2)}) collective-permute-start(bf16[2,2,64,1280]{3,2,1,0:T(8,128)(2,1)S(1)} %bitcast.556), channel_id=1, source_target_pairs={{0,1},{1,0},{2,3},{3,2},{4,5},{5,4},{6,7},{7,6},{8,9},{9,8},{10,11... | collective-permute-start | bytes 1966088 | tf_op jit(solution)/shard_map/ppermute | solution.py:21
  166.2 31.3 %collective-permute-start.8 = (bf16[2,2,64,1280]{3,2,1,0:T(8,128)(2,1)S(1)}, bf16[2,2,64,1280]{3,2,1,0:T(8,128)(2,1)S(1)}, u32[]{:S(2)}, u32[]{:S(2)}) collective-permute-start(bf16[2,2,64,1280]{3,2,1,0:T(8,128)(2,1)S(1)} %bitcast.555), channel_id=1, source_target_pairs={{0,16},{16,0},{1,17},{17,1},{2,18},{18,2},{3,19},{19,3},{4,20},{20... | collective-permute-start | bytes 1966088 | tf_op jit(solution)/shard_map/ppermute | solution.py:21
  172.4 32.1 %collective-permute-start.14 = (bf16[2,2,2,64,1280]{4,3,0,2,1:T(8,128)(2,1)}, bf16[2,2,2,64,1280]{4,3,0,2,1:T(8,128)(2,1)}, u32[]{:S(2)}, u32[]{:S(2)}) collective-permute-start(bf16[2,2,2,64,1280]{4,3,0,2,1:T(8,128)(2,1)} %get-tuple-element.195), channel_id=1, source_target_pairs={{0,16},{16,0},{1,17},{17,1},{2,18},{18,2},{3,19},{19,3},{4,20},{20... | collective-permute-start | bytes 3932168 | tf_op jit(solution)/shard_map/ppermute | solution.py:21
  175.4 31.1 %collective-permute-start.16 = (bf16[2,2,2,64,1280]{4,3,0,2,1:T(8,128)(2,1)}, bf16[2,2,2,64,1280]{4,3,0,2,1:T(8,128)(2,1)}, u32[]{:S(2)}, u32[]{:S(2)}) collective-permute-start(bf16[2,2,2,64,1280]{4,3,0,2,1:T(8,128)(2,1)} %get-tuple-element.199), channel_id=1, source_target_pairs={{0,1},{1,0},{2,3},{3,2},{4,5},{5,4},{6,7},{7,6},{8,9},{9,8},{10,11... | collective-permute-start | bytes 3932168 | tf_op jit(solution)/shard_map/ppermute | solution.py:21
  194.1 40.4 %collective-permute-start.21 = (bf16[2,2,80,2048]{3,2,1,0:T(8,128)(2,1)}, bf16[2,2,80,2048]{3,2,1,0:T(8,128)(2,1)}, u32[]{:S(2)}, u32[]{:S(2)}) collective-permute-start(bf16[2,2,80,2048]{3,2,1,0:T(8,128)(2,1)} %pad_maximum_fusion.26), channel_id=1, source_target_pairs={{0,1},{1,0},{2,3},{3,2},{4,5},{5,4},{6,7},{7,6},{8,9},{9,8},{10,11... | collective-permute-start | bytes 3932168 | tf_op jit(solution)/shard_map/ppermute | solution.py:21
  196.7 57.4 %collective-permute-start.7 = (bf16[2,2,2,64,1280]{4,3,2,1,0:T(8,128)(2,1)}, bf16[2,2,2,64,1280]{4,3,2,1,0:T(8,128)(2,1)}, u32[]{:S(2)}, u32[]{:S(2)}) collective-permute-start(bf16[2,2,2,64,1280]{4,3,2,1,0:T(8,128)(2,1)} %get-tuple-element.201), channel_id=1, source_target_pairs={{0,16},{16,0},{1,17},{17,1},{2,18},{18,2},{3,19},{19,3},{4,20},{20... | collective-permute-start | bytes 3932168 | tf_op jit(solution)/shard_map/ppermute | solution.py:21
  199.2 63.5 %collective-permute-start.9 = (bf16[2,2,2,64,1280]{4,3,2,1,0:T(8,128)(2,1)}, bf16[2,2,2,64,1280]{4,3,2,1,0:T(8,128)(2,1)}, u32[]{:S(2)}, u32[]{:S(2)}) collective-permute-start(bf16[2,2,2,64,1280]{4,3,2,1,0:T(8,128)(2,1)} %get-tuple-element.205), channel_id=1, source_target_pairs={{0,1},{1,0},{2,3},{3,2},{4,5},{5,4},{6,7},{7,6},{8,9},{9,8},{10,11... | collective-permute-start | bytes 3932168 | tf_op jit(solution)/shard_map/ppermute | solution.py:21
  246.4 48.4 %collective-permute-start.22 = (bf16[2,2,2,80,2048]{4,3,2,1,0:T(8,128)(2,1)S(1)}, bf16[2,2,2,80,2048]{4,3,2,1,0:T(8,128)(2,1)S(1)}, u32[]{:S(2)}, u32[]{:S(2)}) collective-permute-start(bf16[2,2,2,80,2048]{4,3,2,1,0:T(8,128)(2,1)S(1)} %pad_maximum_fusion.14), channel_id=1, source_target_pairs={{0,16},{16,0},{1,17},{17,1},{2,18},{18,2},{3,19},{19,3},{4,20},{20... | collective-permute-start | bytes 7864328 | tf_op jit(solution)/shard_map/ppermute | solution.py:21
  251.9 38.5 %collective-permute-start.17 = (f32[1280]{0:T(1024)S(1)}, f32[1280]{0:T(1024)S(1)}, u32[]{:S(2)}, u32[]{:S(2)}) collective-permute-start(f32[1280]{0:T(1024)S(1)} %add_reduce_fusion), channel_id=1, source_target_pairs={{0,16},{1,17},{2,18},{3,19},{4,20},{5,21},{6,22},{7,23},{8,24},{9,... | collective-permute-start | bytes 15368 | tf_op jit(solution)/shard_map/ppermute | solution.py:27
  297.2 26.3 %collective-permute-start.23 = (f32[128,2048]{1,0:T(8,128)}, f32[128,2048]{1,0:T(8,128)}, u32[]{:S(2)}, u32[]{:S(2)}) collective-permute-start(f32[128,2048]{1,0:T(8,128)} %dynamic-slice_bitcast_fusion), channel_id=1, source_target_pairs={{0,8},{8,0},{1,9},{9,1},{2,10},{10,2},{3,11},{11,3},{4,12},{12,4},... | collective-permute-start | bytes 3145736 | tf_op jit(solution)/shard_map/ppermute | solution.py:21
  314.7 401.8 %reduce-scatter.8.cloned.1.call-start = ((), (), s32[]{:S(2)}) async-start(), calls=%async_computation.11 | async-start | bytes 3932160 | tf_op jit(solution)/shard_map/reduce_scatter | solution.py:354
  340.5 23.7 %collective-permute-start.25 = (bf16[2,64,2048]{2,1,0:T(8,128)(2,1)S(1)}, bf16[2,64,2048]{2,1,0:T(8,128)(2,1)S(1)}, u32[]{:S(2)}, u32[]{:S(2)}) collective-permute-start(bf16[2,64,2048]{2,1,0:T(8,128)(2,1)S(1)} %get-tuple-element.243), channel_id=1, source_target_pairs={{0,1},{1,0},{2,3},{3,2},{4,5},{5,4},{6,7},{7,6},{8,9},{9,8},{10,11... | collective-permute-start | bytes 1572872 | tf_op jit(solution)/shard_map/ppermute | solution.py:21
  342.3 22.0 %collective-permute-start.27 = (bf16[2,64,2048]{2,1,0:T(8,128)(2,1)S(1)}, bf16[2,64,2048]{2,1,0:T(8,128)(2,1)S(1)}, u32[]{:S(2)}, u32[]{:S(2)}) collective-permute-start(bf16[2,64,2048]{2,1,0:T(8,128)(2,1)S(1)} %get-tuple-element.249), channel_id=1, source_target_pairs={{0,16},{16,0},{1,17},{17,1},{2,18},{18,2},{3,19},{19,3},{4,20},{20... | collective-permute-start | bytes 1572872 | tf_op jit(solution)/shard_map/ppermute | solution.py:21
  406.4 313.5 %reduce-scatter.6.cloned.1.call-start = ((), (), s32[]{:S(2)}) async-start(), calls=%async_computation.10 | async-start | bytes 3932160 | tf_op jit(solution)/shard_map/reduce_scatter | solution.py:354
  429.9 291.2 %reduce-scatter.4.cloned.1.call-start = ((), (), s32[]{:S(2)}) async-start(), calls=%async_computation.9 | async-start | bytes 3932160 | tf_op jit(solution)/shard_map/reduce_scatter | solution.py:354
  485.0 213.1 %collective-permute-start.65 = (bf16[640,2048]{1,0:T(8,128)(2,1)}, bf16[640,2048]{1,0:T(8,128)(2,1)}, u32[]{:S(2)}, u32[]{:S(2)}) collective-permute-start(bf16[640,2048]{1,0:T(8,128)(2,1)} %convolution_convert_fusion.3), channel_id=1, source_target_pairs={{0,16},{16,0},{1,17},{17,1},{2,18},{18,2},{3,19},{19,3},{4,20},{20... | collective-permute-start | bytes 7864328 | tf_op jit(solution)/shard_map/ppermute | solution.py:21
  488.4 140.2 %collective-permute-start.60 = (bf16[512,1280]{1,0:T(8,128)(2,1)}, bf16[512,1280]{1,0:T(8,128)(2,1)}, u32[]{:S(2)}, u32[]{:S(2)}) collective-permute-start(bf16[512,1280]{1,0:T(8,128)(2,1)} %pad_maximum_fusion.29), channel_id=1, source_target_pairs={{0,1},{1,0},{2,3},{3,2},{4,5},{5,4},{6,7},{7,6},{8,9},{9,8},{10,11... | collective-permute-start | bytes 3932168 | tf_op jit(solution)/shard_map/ppermute | solution.py:21
  489.3 143.0 %collective-permute-start.58 = (bf16[512,1280]{1,0:T(8,128)(2,1)}, bf16[512,1280]{1,0:T(8,128)(2,1)}, u32[]{:S(2)}, u32[]{:S(2)}) collective-permute-start(bf16[512,1280]{1,0:T(8,128)(2,1)} %convolution_convert_fusion.4), channel_id=1, source_target_pairs={{0,16},{16,0},{1,17},{17,1},{2,18},{18,2},{3,19},{19,3},{4,20},{20... | collective-permute-start | bytes 3932168 | tf_op jit(solution)/shard_map/ppermute | solution.py:21
  530.4 41.3 %collective-permute-start.49 = (f32[3,1280]{1,0:T(4,128)S(1)}, f32[3,1280]{1,0:T(4,128)S(1)}, u32[]{:S(2)}, u32[]{:S(2)}) collective-permute-start(f32[3,1280]{1,0:T(4,128)S(1)} %slice.517), channel_id=1, source_target_pairs={{16,0},{17,1},{18,2},{19,3},{20,4},{21,5},{22,6},{23,7},{24,8},{25... | collective-permute-start | bytes 46088 | tf_op jit(solution)/shard_map/ppermute | solution.py:27
  534.5 56.1 %collective-permute-start.70 = (bf16[640,512]{1,0:T(8,128)(2,1)}, bf16[640,512]{1,0:T(8,128)(2,1)}, u32[]{:S(2)}, u32[]{:S(2)}) collective-permute-start(bf16[640,512]{1,0:T(8,128)(2,1)} %fusion.38), channel_id=1, source_target_pairs={{0,16},{16,0},{1,17},{17,1},{2,18},{18,2},{3,19},{19,3},{4,20},{20... | collective-permute-start | bytes 1966088 | tf_op jit(solution)/shard_map/ppermute | solution.py:21
  602.4 92.2 %collective-permute-start.43 = (bf16[512,2048]{1,0:T(8,128)(2,1)}, bf16[512,2048]{1,0:T(8,128)(2,1)}, u32[]{:S(2)}, u32[]{:S(2)}) collective-permute-start(bf16[512,2048]{1,0:T(8,128)(2,1)} %slice.703), channel_id=1, source_target_pairs={{0,8},{8,0},{1,9},{9,1},{2,10},{10,2},{3,11},{11,3},{4,12},{12,4},... | collective-permute-start | bytes 6291464 | tf_op jit(solution)/shard_map/ppermute | solution.py:21
  625.4 35.4 %collective-permute-start.53 = (bf16[512,1280]{1,0:T(8,128)(2,1)}, bf16[512,1280]{1,0:T(8,128)(2,1)}, u32[]{:S(2)}, u32[]{:S(2)}) collective-permute-start(bf16[512,1280]{1,0:T(8,128)(2,1)} %pad_maximum_fusion.28), channel_id=1, source_target_pairs={{0,1},{1,0},{2,3},{3,2},{4,5},{5,4},{6,7},{7,6},{8,9},{9,8},{10,11... | collective-permute-start | bytes 3932168 | tf_op jit(solution)/shard_map/ppermute | solution.py:21
  628.6 34.2 %collective-permute-start.51 = (bf16[512,1280]{1,0:T(8,128)(2,1)}, bf16[512,1280]{1,0:T(8,128)(2,1)S(1)}, u32[]{:S(2)}, u32[]{:S(2)}) collective-permute-start(bf16[512,1280]{1,0:T(8,128)(2,1)} %convolution_convert_fusion.5), channel_id=1, source_target_pairs={{0,16},{16,0},{1,17},{17,1},{2,18},{18,2},{3,19},{19,3},{4,20},{20... | collective-permute-start | bytes 3932168 | tf_op jit(solution)/shard_map/ppermute | solution.py:21
  632.3 27.9 %collective-permute-start.74 = (bf16[80,512]{1,0:T(8,128)(2,1)S(1)}, bf16[80,512]{1,0:T(8,128)(2,1)S(1)}, u32[]{:S(2)}, u32[]{:S(2)}) collective-permute-start(bf16[80,512]{1,0:T(8,128)(2,1)S(1)} %fusion.109), channel_id=1, source_target_pairs={{0,0},{16,8},{8,16},{24,24},{1,1},{17,9},{9,17},{25,25},{2,2},{18,... | collective-permute-start | bytes 245768 | tf_op jit(solution)/shard_map/ppermute | solution.py:128
  665.4 24.2 %collective-permute-start.54 = (bf16[2,2,64,1280]{3,2,1,0:T(8,128)(2,1)S(1)}, bf16[2,2,64,1280]{3,2,1,0:T(8,128)(2,1)S(1)}, u32[]{:S(2)}, u32[]{:S(2)}) collective-permute-start(bf16[2,2,64,1280]{3,2,1,0:T(8,128)(2,1)S(1)} %bitcast.571), channel_id=1, source_target_pairs={{0,16},{16,0},{1,17},{17,1},{2,18},{18,2},{3,19},{19,3},{4,20},{20... | collective-permute-start | bytes 1966088 | tf_op jit(solution)/shard_map/ppermute | solution.py:21
  678.8 32.2 %collective-permute-start.62 = (bf16[2,2,64,1280]{3,2,0,1:T(8,128)(2,1)S(1)}, bf16[2,2,64,1280]{3,2,0,1:T(8,128)(2,1)S(1)}, u32[]{:S(2)}, u32[]{:S(2)}) collective-permute-start(bf16[2,2,64,1280]{3,2,0,1:T(8,128)(2,1)S(1)} %fusion.64), channel_id=1, source_target_pairs={{0,2},{2,0},{1,3},{3,1},{4,6},{6,4},{5,7},{7,5},{8,10},{10,8},{9,1... | collective-permute-start | bytes 1966088 | tf_op jit(solution)/shard_map/ppermute | solution.py:21
  692.9 22.1 %collective-permute-start.55 = (bf16[2,2,64,1280]{3,2,0,1:T(8,128)(2,1)S(1)}, bf16[2,2,64,1280]{3,2,0,1:T(8,128)(2,1)S(1)}, u32[]{:S(2)}, u32[]{:S(2)}) collective-permute-start(bf16[2,2,64,1280]{3,2,0,1:T(8,128)(2,1)S(1)} %fusion.63), channel_id=1, source_target_pairs={{0,2},{2,0},{1,3},{3,1},{4,6},{6,4},{5,7},{7,5},{8,10},{10,8},{9,1... | collective-permute-start | bytes 1966088 | tf_op jit(solution)/shard_map/ppermute | solution.py:21
  703.4 58.4 %collective-permute-start.66 = (bf16[2,2,80,2048]{3,2,0,1:T(8,128)(2,1)}, bf16[2,2,80,2048]{3,2,0,1:T(8,128)(2,1)}, u32[]{:S(2)}, u32[]{:S(2)}) collective-permute-start(bf16[2,2,80,2048]{3,2,0,1:T(8,128)(2,1)} %fusion.30), channel_id=1, source_target_pairs={{0,1},{1,0},{2,3},{3,2},{4,5},{5,4},{6,7},{7,6},{8,9},{9,8},{10,11... | collective-permute-start | bytes 3932168 | tf_op jit(solution)/shard_map/ppermute | solution.py:21
  710.1 32.6 %collective-permute-start.47 = (bf16[64,2048]{1,0:T(8,128)(2,1)}, bf16[64,2048]{1,0:T(8,128)(2,1)}, u32[]{:S(2)}, u32[]{:S(2)}) collective-permute-start(bf16[64,2048]{1,0:T(8,128)(2,1)} %fusion.97), channel_id=1, source_target_pairs={{0,1},{1,0},{2,3},{3,2},{4,5},{5,4},{6,7},{7,6},{8,9},{9,8},{10,11... | collective-permute-start | bytes 786440 | tf_op jit(solution)/shard_map/ppermute | solution.py:21
  712.0 33.1 %collective-permute-start.63 = (bf16[2,64,1280]{2,1,0:T(8,128)(2,1)}, bf16[2,64,1280]{2,1,0:T(8,128)(2,1)}, u32[]{:S(2)}, u32[]{:S(2)}) collective-permute-start(bf16[2,64,1280]{2,1,0:T(8,128)(2,1)} %fusion.85), channel_id=1, source_target_pairs={{0,4},{4,0},{1,5},{5,1},{2,6},{6,2},{3,7},{7,3},{8,12},{12,8},{9,1... | collective-permute-start | bytes 983048 | tf_op jit(solution)/shard_map/ppermute | solution.py:21
  716.3 30.9 %collective-permute-start.56 = (bf16[2,64,1280]{2,1,0:T(8,128)(2,1)}, bf16[2,64,1280]{2,1,0:T(8,128)(2,1)}, u32[]{:S(2)}, u32[]{:S(2)}) collective-permute-start(bf16[2,64,1280]{2,1,0:T(8,128)(2,1)} %fusion.84), channel_id=1, source_target_pairs={{0,4},{4,0},{1,5},{5,1},{2,6},{6,2},{3,7},{7,3},{8,12},{12,8},{9,1... | collective-permute-start | bytes 983048 | tf_op jit(solution)/shard_map/ppermute | solution.py:21
  718.5 36.8 %collective-permute-start.77 = (bf16[256,768]{1,0:T(8,128)(2,1)}, bf16[256,768]{1,0:T(8,128)(2,1)S(1)}, u32[]{:S(2)}, u32[]{:S(2)}) collective-permute-start(bf16[256,768]{1,0:T(8,128)(2,1)} %fusion.77), channel_id=1, source_target_pairs={{0,1},{1,0},{2,3},{3,2},{4,5},{5,4},{6,7},{7,6},{8,9},{9,8},{10,11... | collective-permute-start | bytes 1179656 | tf_op jit(solution)/shard_map/ppermute | solution.py:21
  745.1 22.8 %collective-permute-start.75 = (bf16[256,768]{1,0:T(8,128)(2,1)S(1)}, bf16[256,768]{1,0:T(8,128)(2,1)S(1)}, u32[]{:S(2)}, u32[]{:S(2)}) collective-permute-start(bf16[256,768]{1,0:T(8,128)(2,1)S(1)} %fusion.75), channel_id=1, source_target_pairs={{0,1},{1,0},{2,3},{3,2},{4,5},{5,4},{6,7},{7,6},{8,9},{9,8},{10,11... | collective-permute-start | bytes 1179656 | tf_op jit(solution)/shard_map/ppermute | solution.py:21
  755.4 24.5 %collective-permute-start.57 = (f32[64,1280]{1,0:T(8,128)}, f32[64,1280]{1,0:T(8,128)}, u32[]{:S(2)}, u32[]{:S(2)}) collective-permute-start(f32[64,1280]{1,0:T(8,128)} %dynamic-slice_bitcast_fusion.2), channel_id=1, source_target_pairs={{0,8},{8,0},{1,9},{9,1},{2,10},{10,2},{3,11},{11,3},{4,12},{12,4},... | collective-permute-start | bytes 983048 | tf_op jit(solution)/shard_map/ppermute | solution.py:21
  (155 other events, 1620.3 us)
Sparse Core Ops, SparseCore 0:
  24.8 73.0 all-gather.4
  99.5 92.7 all-gather.8
  193.9 63.3 all-gather.6
  314.9 67.3 all-gather.10
  406.5 62.1 reduce-scatter.7
  470.8 60.2 reduce-scatter.5
  533.4 60.2 reduce-scatter.3
